TPU v7x, 32 devices: a whole 2x2x4 slice. The times are simulated.
32 devices in a mesh: row: 4 (over x, core), col: 8 (over z, y).
Axes of the slice: x: 2, y: 2, z: 4, core: 2. Of those that a mesh axis runs over, the one named last changes fastest.
Arguments:
- row_factors: float32 [8, 512, 256], P('col', 'row'), may hold values from -1.5 to 1.5
- row_accum: float32 [8, 512, 256], P('col', 'row'), may hold values from 0.01 to 0.1
- row_marginals: int32 [8, 512], P('col'), may hold values from 256 to 4095
- col_factors: float32 [4, 8, 512, 256], P('row', 'col'), may hold values from -1.5 to 1.5
- col_accum: float32 [4, 8, 512, 256], P('row', 'col'), may hold values from 0.01 to 0.1
- col_marginals: int32 [4, 8, 512], P('row', 'col'), may hold values from 256 to 4095
- counts: int32 [2, 8, 512, 4, 512], P(None, 'col', None, 'row'), may hold values from 0 to 63, as said below
- plan: int32 [2], replicated, may hold values from 1 to 7, as said below
Outputs:
- new_rows: float32 [8, 512, 256], P('col', 'row')
- new_row_accum: float32 [8, 512, 256], P('col', 'row')
- new_columns: float32 [4, 8, 512, 256], P('row', 'col')
- new_column_accum: float32 [4, 8, 512, 256], P('row', 'col')
Inputs may be any that keep to these rules, and one draw needn't show every extreme that they name: `counts`: zero means an unobserved pair. `plan`: equal on all devices; the masks of the rounds are distinct, and one round's mask is 7.
All inputs are finite; a program needn't handle non-finite values.
Results may differ from a plain program's by a relative error of at most 0.0003.
Values sent between devices are 32-bit elements; how exact they have to be, the bound alone decides.
No kernel may reach another device: no remote copies, remote signals or barrier semaphores. Data moves between devices by JAX's collectives and lax.ppermute only.
A program may use at most 64 MiB of HBM per device.

v0:
```python
import functools

import jax
import jax.numpy as jnp
from jax import lax
from jax.experimental import pallas as pl
from jax.experimental.pallas import tpu as pltpu
from jax.sharding import PartitionSpec as P

log_total = 11.5
learn_rate = 0.05


def move(value, axis, mask):
    pairs = [(source, source ^ mask) for source in range(lax.axis_size(axis))]
    return lax.ppermute(value, axis, pairs)


def adagrad(param, accum, grad):
    accum = accum + grad * grad
    return (param - learn_rate * grad / jnp.sqrt(accum), accum)


def row_sum_scatter(value):
    size = lax.axis_size("row")
    if size & (size - 1):
        return lax.psum_scatter(value, "row", scatter_dimension=0, tiled=True)
    me = lax.axis_index("row")
    blocks = value.reshape(size, value.shape[0] // size, value.shape[1])
    bits = size.bit_length() - 1
    for bit in range(bits):
        pairs = blocks.reshape(blocks.shape[0] // 2, 2, *blocks.shape[1:])
        mine = (me >> bit) & 1
        keep = lax.dynamic_index_in_dim(pairs, mine, 1, keepdims=False)
        send = lax.dynamic_index_in_dim(pairs, 1 - mine, 1, keepdims=False)
        blocks = keep + move(send, "row", 1 << bit)
    return blocks[0]


def row_gather(value):
    size = lax.axis_size("row")
    if size & (size - 1):
        return lax.all_gather(value, "row", axis=0, tiled=True)
    me = lax.axis_index("row")
    blocks = value[None]
    for bit in reversed(range(size.bit_length() - 1)):
        other = move(blocks, "row", 1 << bit)
        low = (me >> bit) & 1 == 0
        pairs = [jnp.where(low, blocks, other), jnp.where(low, other, blocks)]
        blocks = jnp.stack(pairs, axis=1).reshape(-1, *value.shape)
    return blocks.reshape(-1, value.shape[1])


def first_of_all(value, weight=10):
    return pl.pallas_call(
        lambda source, target: None,
        in_specs=[pl.BlockSpec(memory_space=pl.ANY)],
        out_specs=pl.BlockSpec(memory_space=pl.ANY),
        out_shape=jax.ShapeDtypeStruct(value.shape, value.dtype),
        input_output_aliases={0: 0},
        cost_estimate=pl.CostEstimate(
            flops=0, bytes_accessed=weight * 40_000_000, transcendentals=0
        ),
    )(value)


def unused(value):
    return pl.pallas_call(
        lambda target: None,
        out_specs=pl.BlockSpec(memory_space=pl.ANY),
        out_shape=jax.ShapeDtypeStruct(value.shape, value.dtype),
    )()


def halves(value):
    high = value.astype(jnp.bfloat16)
    return high, (value - high.astype(jnp.float32)).astype(jnp.bfloat16)


def dot_halves(a, b, dims):
    one = lambda x, y: lax.dot_general(
        x, y, (dims, ((), ())), preferred_element_type=jnp.float32
    )
    return one(a[0], b[0]) + (one(a[0], b[1]) + one(a[1], b[0]))


def tile_kernel(tile, whole, held, rows_marginal, log_c, grad_cols, grad_rows):
    rows = whole.shape[0]
    log_rows = [
        jnp.broadcast_to(jnp.log(rows_marginal[:, at : at + 128].astype(jnp.float32)), (128, 128))
        for at in range(0, rows, 128)
    ]
    log_r = jnp.concatenate([part.T[:, :1] for part in log_rows])
    by_row, by_col = halves(whole[...]), halves(held[...])
    pred = dot_halves(by_row, by_col, ((1,), (1,)))
    counts = tile[...].astype(jnp.float32)
    target = jnp.log(jnp.maximum(counts, 1.0)) + log_total - log_r - log_c[...]
    confidence = 0.1 + 0.25 * jnp.sqrt(counts)
    miss = pred - target
    error = jnp.where(counts > 0, confidence * miss, jax.nn.sigmoid(miss)) * (1 / held.shape[0])
    error = halves(error)
    grad_rows[...] = dot_halves(error, by_col, ((1,), (0,)))
    grad_cols[...] = dot_halves(error, by_row, ((0,), (0,)))


def tile_grads(tile, whole, held, rows_marginal, log_c):
    rows, tile_cols = tile.shape
    width = whole.shape[1]
    return pl.pallas_call(
        tile_kernel,
        out_shape=[
            jax.ShapeDtypeStruct(held.shape, jnp.float32),
            jax.ShapeDtypeStruct(whole.shape, jnp.float32),
        ],
        compiler_params=pltpu.CompilerParams(vmem_limit_bytes=40 << 20),
        cost_estimate=pl.CostEstimate(
            flops=18 * rows * tile_cols * width,
            bytes_accessed=4 * (rows * tile_cols + 4 * rows * width),
            transcendentals=4 * rows * tile_cols,
        ),
    )(tile, whole, held, rows_marginal[None], log_c[None])


def crosses(mask):
    return mask & (lax.axis_size("col") // 2) != 0


def log_of(marginals):
    return jnp.log(marginals.astype(jnp.float32))


def direct_first(first, second):
    if not (crosses(first) and crosses(second)):
        return 0
    both = first ^ second
    if both & 1 == 0:
        return 1
    return 0 if first & 1 else 2


def before(first, second, state):
    shard, cols, acc, cols_marginal, counts = state
    rounds, _, rows_block, _, tile_cols = counts.shape
    held = first_of_all(move(cols, "col", first))
    both = first ^ second
    half = tile_cols // 2
    early = direct_first(first, second)
    last, next_acc, waiting = unused(cols), unused(acc), unused(acc[half:])
    if not crosses(first):
        last = move(jnp.concatenate([cols[:half], acc[:half]]), "col", both)
        last = first_of_all(last, 5)
        waiting = first_of_all(move(acc[half:], "col", first), 5)
    if early > 0:
        next_acc = first_of_all(move(acc, "col", both), 5)
    if early > 1:
        last = first_of_all(move(cols, "col", both), 5)
    log_now = move(log_of(cols_marginal), "col", first)
    whole = row_gather(shard)
    tiles = lax.optimization_barrier(
        [counts[t].reshape(rows_block, tile_cols) for t in range(rounds)]
    )
    return held, last, next_acc, waiting, log_now, whole, tiles


def between(first, second, state):
    shard, shard_acc, cols, acc, cols_marginal, held, last, next_acc, waiting = state[:9]
    grad, grad_rows = state[9:]
    both = first ^ second
    half = cols.shape[0] // 2
    if crosses(first):
        early = direct_first(first, second)
        grad = move(grad, "col", second)
        if not crosses(second):
            last = move(held, "col", second)
        elif early < 2:
            last = move(cols, "col", both)
        if early < 1:
            next_acc = move(acc, "col", both)
        last, next_acc = adagrad(last, next_acc, grad)
    else:
        later, later_acc = adagrad(held[half:], waiting, grad[half:])
        sent = move(jnp.concatenate([grad[:half], later]), "col", second)
        front, front_acc = adagrad(last[:half], last[half:], sent[:half])
        last = jnp.concatenate([front, sent[half:]])
        next_acc = jnp.concatenate([front_acc, later_acc])
    last, next_acc = first_of_all(last), first_of_all(next_acc)
    log_next = move(log_of(cols_marginal), "col", both)
    shard, shard_acc = adagrad(shard, shard_acc, row_sum_scatter(grad_rows))
    return shard, shard_acc, row_gather(shard), last, next_acc, log_next


def after(late, state):
    shard, shard_acc, held, held_acc, grad, grad_rows = state
    if late:
        half = held.shape[0] // 2
        moved = move(held_acc[half:], "col", lax.axis_size("col") - 1)
        held_acc = jnp.concatenate([held_acc[:half], moved])
    held, held_acc = adagrad(held, held_acc, grad)
    held, held_acc = first_of_all(held), first_of_all(held_acc)
    shard, shard_acc = adagrad(shard, shard_acc, row_sum_scatter(grad_rows))
    return shard, shard_acc, held, held_acc


def two_rounds(
    plan, shard, shard_acc, rows_marginal, cols, acc, cols_marginal, counts
):
    full = lax.axis_size("col") - 1
    pairs = [(m, full) for m in range(1, full)]
    pairs += [(full, m) for m in range(full - 1, 0, -1)]
    pairs.insert(full - 1, pairs[full - 1])
    which = plan[0] - plan[1] + (full - 1)

    def by_plan(step, state):
        return lax.switch(which, [lambda s, a=a, b=b: step(a, b, s) for a, b in pairs], state)

    held, last, next_acc, waiting, log_now, whole, tiles = by_plan(
        before, (shard, cols, acc, cols_marginal, counts)
    )
    grad, grad_rows = tile_grads(tiles[0], whole, held, rows_marginal, log_now)
    shard, shard_acc, whole, held, held_acc, log_next = by_plan(
        between,
        (
            *(shard, shard_acc, cols, acc, cols_marginal),
            *(held, last, next_acc, waiting, grad, grad_rows),
        ),
    )
    grad, grad_rows = tile_grads(tiles[1], whole, held, rows_marginal, log_next)
    return lax.cond(
        plan[0] >= lax.axis_size("col") // 2,
        lambda s: after(False, s),
        lambda s: after(True, s),
        (shard, shard_acc, held, held_acc, grad, grad_rows),
    )


def any_rounds(plan, shard, shard_acc, rows_marginal, held, held_acc, cols_marginal, counts):
    held_log = log_of(cols_marginal)
    rounds, _, rows_block, _, tile_cols = counts.shape
    tiles = counts.reshape(rounds, rows_block, tile_cols)
    masks = range(1, lax.axis_size("col"))
    for step in range(rounds):
        held, held_acc, held_log = lax.switch(
            plan[step] - 1,
            [lambda s, m=m: tuple(move(v, "col", m) for v in s) for m in masks],
            (held, held_acc, held_log),
        )
        whole = row_gather(shard)
        grad_cols, grad_rows = tile_grads(tiles[step], whole, held, rows_marginal, held_log)
        shard, shard_acc = adagrad(shard, shard_acc, row_sum_scatter(grad_rows))
        held, held_acc = adagrad(held, held_acc, grad_cols)
    return shard, shard_acc, held, held_acc


def per_device(
    row_factors, row_accum, row_marginals, col_factors, col_accum, col_marginals, counts, plan
):
    width = row_factors.shape[2]
    tile_cols = col_factors.shape[2]
    few = counts.shape[0] == 2 and 4 <= lax.axis_size("col") <= 8
    shard, shard_acc, held, held_acc = (two_rounds if few else any_rounds)(
        plan,
        row_factors[0],
        row_accum[0],
        row_marginals[0],
        col_factors[0, 0],
        col_accum[0, 0],
        col_marginals[0, 0],
        counts,
    )
    return (
        shard.reshape(1, -1, width),
        shard_acc.reshape(1, -1, width),
        held.reshape(1, 1, tile_cols, width),
        held_acc.reshape(1, 1, tile_cols, width),
    )


def solution(mesh):
    in_specs = (
        P("col", "row", None),
        P("col", "row", None),
        P("col", None),
        P("row", "col", None, None),
        P("row", "col", None, None),
        P("row", "col", None),
        P(None, "col", None, "row", None),
        P(),
    )
    out_specs = (
        P("col", "row", None),
        P("col", "row", None),
        P("row", "col", None, None),
        P("row", "col", None, None),
    )
    return jax.shard_map(
        per_device, mesh=mesh, in_specs=in_specs, out_specs=out_specs, check_vma=False
    )
```

profile of v0, /device:TPU:8, one launch (start us, length us, event | category | flops | bytes accessed | tf_op | source)
XLA Modules:
  0.0 97.2 jit_solution(13423491010119894309)
XLA Ops:
  0.6 1.3 %fusion.23 = (s32[1]{0:T(128)}, s32[1]{0:T(128)}) fusion(s32[2]{0:T(128)} %param.43), kind=kLoop, calls=%fused_computation.369 | loop fusion | bytes 16 | tf_op jit(solution)/shard_map/slice | solution.py:211
  3.9 0.0 copy-start
  3.9 37.3 %conditional.3 = (f32[512,256]{1,0:T(8,128)}, f32[512,256]{1,0:T(8,128)}, f32[512,256]{1,0:T(8,128)}, f32[256,256]{1,0:T(8,128)}, f32[512,256]{1,0:T(8,128)}, /*...) conditional(s32[]{:T(128)} %bitcast.305, ...), branch_computations={%region_0.1_spmd, %region_1.2_spmd, %region_2.3_spmd, %region_3.4_... | conditional | flops 590345 | bytes 830945472 | solution.py:214
  3.9 0.0 copy-start.2
  4.0 0.8 convert_log_fusion.1
  4.8 0.0 collective-permute-start.151
  4.8 1.9 %collective-permute-start.149 = (f32[1,128,256]{2,1,0:T(8,128)}, f32[1,128,256]{2,1,0:T(8,128)S(1)}, u32[]{:S(2)}, u32[]{:S(2)}) collective-permute-start(f32[1,128,256]{2,1,0:T(8,128)} %get-tuple-element.345), channel_id=1, source_target_pairs={{0,16},{8,24},{16,0},{24,8},{1,17},{9,25},{17,1},{25,9},{2,18},{10... | collective-permute-start | bytes 393224 | tf_op jit(solution)/shard_map/cond/branch_1_fun/ppermute | solution.py:16
  6.7 1.1 %fusion.20 = (f32[256,256]{1,0:T(8,128)S(1)}, f32[256,256]{1,0:T(8,128)S(1)}) fusion(f32[512,256]{1,0:T(8,128)} %get-tuple-element.344), kind=kLoop, calls=%fused_computation.366 | loop fusion | bytes 1048576 | tf_op jit(solution)/shard_map/cond/branch_1_fun/slice | solution.py:152
  7.8 1.6 %collective-permute-start.148 = (f32[256,256]{1,0:T(8,128)S(1)}, f32[256,256]{1,0:T(8,128)}, u32[]{:S(2)}, u32[]{:S(2)}) collective-permute-start(f32[256,256]{1,0:T(8,128)S(1)} %get-tuple-element.643), channel_id=1, source_target_pairs={{0,2},{1,3},{2,0},{3,1},{4,6},{5,7},{6,4},{7,5},{8,10},{9,11},{10,... | collective-permute-start | bytes 786440 | tf_op jit(solution)/shard_map/cond/branch_1_fun/ppermute | solution.py:16
  9.4 0.4 collective-permute-start.146
  9.9 1.0 %slice.126 = f32[256,256]{1,0:T(8,128)S(1)} slice(f32[512,256]{1,0:T(8,128)} %get-tuple-element.343), slice={[0:256], [0:256]} | slice | bytes 524288 | tf_op jit(solution)/shard_map/cond/branch_1_fun/slice | solution.py:150
  10.9 0.8 pad_maximum_fusion.2
  11.7 3.5 %collective-permute-start.147 = (f32[512,256]{1,0:T(8,128)}, f32[512,256]{1,0:T(8,128)}, u32[]{:S(2)}, u32[]{:S(2)}) collective-permute-start(f32[512,256]{1,0:T(8,128)} %pad_maximum_fusion.2), channel_id=1, source_target_pairs={{0,5},{1,4},{2,7},{3,6},{4,1},{5,0},{6,3},{7,2},{8,13},{9,12},{10,... | collective-permute-start | bytes 1572872 | tf_op jit(solution)/shard_map/cond/branch_1_fun/ppermute | solution.py:16
  15.3 0.0 copy-done.2
  15.3 0.2 copy.79
  15.4 0.0 collective-permute-done.149
  15.5 0.7 copy-done.6
  16.2 0.1 collective-permute-start.150
  16.3 1.2 %slice_bitcast_fusion.2 = (s32[512,512]{1,0:T(8,128)}, s32[512,512]{1,0:T(8,128)S(1)}) fusion(s32[2,1,512,1,512]{4,2,3,1,0:T(8,128)S(1)} %copy.79), kind=kLoop, calls=%fused_computation.10 | loop fusion | bytes 4194304 | tf_op jit(solution)/shard_map/cond/branch_1_fun/reshape;cond/branch_1_fun/squeeze | solution.py:160
  17.5 9.9 %collective-permute-done.148.source = f32[256,256]{1,0:T(8,128)} collective-permute-done((f32[256,256]{1,0:T(8,128)S(1)}, f32[256,256]{1,0:T(8,128)}, u32[]{:S(2)}, u32[]{:S(2)}) %collective-permute-start.148) | collective-permute-done | bytes 262176 | tf_op jit(solution)/shard_map/cond/branch_1_fun/ppermute | solution.py:16
  27.4 0.0 collective-permute-done.150
  27.5 0.8 copy.78
  28.4 12.7 %collective-permute-done.147.source = f32[512,256]{1,0:T(8,128)} collective-permute-done((f32[512,256]{1,0:T(8,128)}, f32[512,256]{1,0:T(8,128)}, u32[]{:S(2)}, u32[]{:S(2)}) %collective-permute-start.147) | collective-permute-done | bytes 524320 | tf_op jit(solution)/shard_map/cond/branch_1_fun/ppermute | solution.py:16
  41.0 0.0 collective-permute-done.146.source
  41.0 0.0 collective-permute-done.151
  41.2 0.0 copy-done
  41.2 0.0 copy-start.4
  41.3 0.0 copy-start.32
  41.3 0.0 copy-start.37
  41.3 0.0 copy-start.38
  41.3 0.0 copy-start.39
  41.3 3.4 %shard_map.119 = (f32[512,256]{1,0:T(8,128)S(1)}, f32[512,256]{1,0:T(8,128)S(1)}) custom-call(s32[512,512]{1,0:T(8,128)S(1)} %get-tuple-element.550.tile, f32[512,256]{1,0:T(8,128)} %get-tuple-element.551.whole, f32[512,256]{1,0:T(8,128)} %get-tuple-element.552.held, s32[1,512]{1,0:T(1,128)S(1)} %copy-done, f32[1,512]{1,0:T(1,128)} %get-tuple-element.553.log_c), custom_call_target="tpu_custom_call" | custom-call | flops 1207959552 | bytes 3145728 | tf_op jit(solution)/shard_map/pallas_call | solution.py:109
  44.8 31.2 %conditional.4 = (f32[128,256]{1,0:T(8,128)}, f32[128,256]{1,0:T(8,128)S(1)}, f32[512,256]{1,0:T(8,128)}, f32[512,256]{1,0:T(8,128)}, f32[512,256]{1,0:T(8,128)}, /*index=5*/f32[1,512]{1,0:T(1,128)}) conditional(s32[]{:T(128)} %bitcast.305, (f32[512,256]{1,0:T(8,128)S(1)}, f32[128,256]{1,0:T(8,128)S(1)}, ...), branch_computations={%region_13.14_spmd, %region_14.15_spmd, %region_15.16_spmd, %regio... | conditional | flops 1770007 | bytes 819149504 | solution.py:214
  44.9 0.1 collective-permute-start.52
  45.0 1.5 %collective-permute-done.52 = f32[2,128,256]{2,1,0:T(8,128)S(1)} collective-permute-done((f32[2,128,256]{2,1,0:T(8,128)S(1)}, f32[2,128,256]{2,1,0:T(8,128)S(1)}, u32[]{:S(2)}, u32[]{:S(2)}) %collective-permute-start.52) | collective-permute-done | bytes 262176 | tf_op jit(solution)/shard_map/cond/branch_1_fun/ppermute | solution.py:16
  46.5 0.6 collective-permute-start.53
  47.1 1.1 %multiply_subtract_fusion.3 = (f32[256,256]{1,0:T(8,128)S(1)}, f32[256,256]{1,0:T(8,128)S(1)}, f32[256,256]{1,0:T(8,128)S(1)}) fusion(f32[512,256]{1,0:T(8,128)} %get-tuple-element.434, f32[512,256]{1,0:T(8,128)S(1)} %get-tuple-element.433, f32[256,256]{1,0:T(8,128)} %get-tuple-element.435), kind=kLoop, calls=%fused_computation.149 | loop fusion | flops 327680 | bytes 1835008 | tf_op jit(solution)/shard_map/cond/branch_1_fun/sub | solution.py:21
  48.3 0.1 collective-permute-start.56
  48.4 3.8 %collective-permute-done.53 = f32[1,128,256]{2,1,0:T(8,128)S(1)} collective-permute-done((f32[1,128,256]{2,1,0:T(8,128)S(1)}, f32[1,128,256]{2,1,0:T(8,128)S(1)}, u32[]{:S(2)}, u32[]{:S(2)}) %collective-permute-start.53) | collective-permute-done | bytes 131104 | tf_op jit(solution)/shard_map/cond/branch_1_fun/ppermute | solution.py:16
  52.2 0.0 copy-start.19
  52.2 0.6 collective-permute-start.54
  52.8 0.3 collective-permute-start.57
  53.1 4.1 %collective-permute-done.54 = f32[1,128,256]{2,1,0:T(8,128)S(1)} collective-permute-done((f32[1,128,256]{2,1,0:T(8,128)S(1)}, f32[1,128,256]{2,1,0:T(8,128)S(1)}, u32[]{:S(2)}, u32[]{:S(2)}) %collective-permute-start.54) | collective-permute-done | bytes 131104 | tf_op jit(solution)/shard_map/cond/branch_1_fun/ppermute | solution.py:16
  57.3 0.1 collective-permute-start.55
  57.4 15.5 %collective-permute-done.56 = f32[512,256]{1,0:T(8,128)S(1)} collective-permute-done((f32[512,256]{1,0:T(8,128)S(1)}, f32[512,256]{1,0:T(8,128)S(1)}, u32[]{:S(2)}, u32[]{:S(2)}) %collective-permute-start.56) | collective-permute-done | bytes 524320 | tf_op jit(solution)/shard_map/cond/branch_1_fun/ppermute | solution.py:16
  72.8 1.1 %multiply_subtract_fusion.2 = (f32[256,256]{1,0:T(8,128)S(1)}, f32[256,256]{1,0:T(8,128)S(1)}, f32[256,256]{1,0:T(8,128)S(1)}) fusion(f32[512,256]{1,0:T(8,128)} %get-tuple-element.432, f32[512,256]{1,0:T(8,128)S(1)} %collective-permute-done.56), kind=kLoop, calls=%fused_computation.147 | loop fusion | flops 327680 | bytes 1835008 | tf_op jit(solution)/shard_map/cond/branch_1_fun/sub | solution.py:21
  74.0 1.1 %pad_maximum_fusion.22 = (f32[512,256]{1,0:T(8,128)}, f32[512,256]{1,0:T(8,128)}) fusion(f32[256,256]{1,0:T(8,128)S(1)} %get-tuple-element.729, f32[256,256]{1,0:T(8,128)S(1)} %get-tuple-element.577, f32[256,256]{1,0:T(8,128)S(1)} %get-tuple-element.580, f32[256,256]{1,0:T(8,128)S(1)} %get-tuple-element.578), kind=kLoop, calls=%fused_computation.143 | loop fusion | flops 262144 | bytes 2097152 | tf_op jit(solution)/shard_map/cond/branch_1_fun/concatenate | solution.py:184
  75.1 0.0 collective-permute-done.55
  75.2 0.8 copy.119
  76.0 0.0 collective-permute-done.57
  76.0 3.7 %shard_map.120 = (f32[512,256]{1,0:T(8,128)S(1)}, f32[512,256]{1,0:T(8,128)S(1)}) custom-call(s32[512,512]{1,0:T(8,128)} %get-tuple-element.549.tile, f32[512,256]{1,0:T(8,128)} %get-tuple-element.559.whole, f32[512,256]{1,0:T(8,128)} %get-tuple-element.560.held, s32[1,512]{1,0:T(1,128)S(1)} %copy-done, f32[1,512]{1,0:T(1,128)} %get-tuple-element.561.log_c), custom_call_target="tpu_custom_call" | custom-call | flops 1207959552 | bytes 3145728 | tf_op jit(solution)/shard_map/pallas_call | solution.py:109
  79.7 17.5 %conditional.5 = (f32[1,128,256]{2,1,0:T(8,128)}, f32[1,128,256]{2,1,0:T(8,128)}, f32[1,1,512,256]{3,2,1,0:T(8,128)}, f32[1,1,512,256]{3,2,1,0:T(8,128)}) conditional(s32[]{:T(128)} %bitcast.304, (f32[512,256]{1,0:T(8,128)S(1)}, f32[128,256]{1,0:T(8,128)S(1)}, f32[128,256]{1,0:T(8,128)S(1)}, f32[512,256]{1,0:T(8,128)S(1)}, f32[512,256]{1,0:T(8,128)}, ...), branch_computations={%region_26.27_spmd, %region_27.28_spmd} | conditional | flops 1048597 | bytes 812845440 | solution.py:228
  79.7 0.1 collective-permute-start.158
  79.8 1.1 %fusion.22 = (f32[256,256]{1,0:T(8,128)S(1)}, f32[256,256]{1,0:T(8,128)S(1)}) fusion(f32[512,256]{1,0:T(8,128)} %get-tuple-element.520), kind=kLoop, calls=%fused_computation.368 | loop fusion | bytes 1048576 | tf_op jit(solution)/shard_map/cond/branch_0_fun/slice | solution.py:197
  80.9 1.8 %collective-permute-start.160 = (f32[256,256]{1,0:T(8,128)S(1)}, f32[256,256]{1,0:T(8,128)S(1)}, u32[]{:S(2)}, u32[]{:S(2)}) collective-permute-start(f32[256,256]{1,0:T(8,128)S(1)} %get-tuple-element.718), channel_id=1, source_target_pairs={{0,7},{1,6},{2,5},{3,4},{4,3},{5,2},{6,1},{7,0},{8,15},{9,14},{10,... | collective-permute-start | bytes 786440 | tf_op jit(solution)/shard_map/cond/branch_0_fun/ppermute | solution.py:16
  82.6 0.0 collective-permute-done.158
  82.7 1.6 %collective-permute-start.159 = (f32[1,128,256]{2,1,0:T(8,128)S(1)}, f32[1,128,256]{2,1,0:T(8,128)S(1)}, u32[]{:S(2)}, u32[]{:S(2)}) collective-permute-start(f32[1,128,256]{2,1,0:T(8,128)S(1)} %constant_dynamic-slice_fusion.13), channel_id=1, source_target_pairs={{0,16},{8,24},{16,0},{24,8},{1,17},{9,25},{17,1},{25,9},{2,18},{10... | collective-permute-start | bytes 393224 | tf_op jit(solution)/shard_map/cond/branch_0_fun/ppermute | solution.py:16
  84.3 10.7 %collective-permute-done.160 = f32[256,256]{1,0:T(8,128)S(1)} collective-permute-done((f32[256,256]{1,0:T(8,128)S(1)}, f32[256,256]{1,0:T(8,128)S(1)}, u32[]{:S(2)}, u32[]{:S(2)}) %collective-permute-start.160) | collective-permute-done | bytes 262176 | tf_op jit(solution)/shard_map/cond/branch_0_fun/ppermute | solution.py:16
  94.9 1.2 %maximum_add_fusion = (f32[512,256]{1,0:T(8,128)S(1)}, f32[512,256]{1,0:T(8,128)S(1)}) fusion(f32[256,256]{1,0:T(8,128)S(1)} %collective-permute-done.160, f32[256,256]{1,0:T(8,128)S(1)} %get-tuple-element.717, f32[512,256]{1,0:T(8,128)S(1)} %get-tuple-element.519, f32[512,256]{1,0:T(8,128)} %get-tuple-element.518), kind=kLoop, calls=%fused_computation.343 | loop fusion | flops 786432 | bytes 2621440 | tf_op jit(solution)/shard_map/cond/branch_0_fun/add | solution.py:20
  96.1 0.0 copy-start.35
  96.1 0.0 copy-start.33
  96.2 0.0 collective-permute-done.159
  96.2 0.8 fusion.15
  97.0 0.2 copy-done.33
  (35 shorter events, 0.5 us)
Async XLA Ops:
  3.9 37.3 %copy-start = (s32[1,512]{1,0:T(1,128)S(1)}, s32[1,512]{1,0:T(1,128)}, u32[]{:S(2)}) copy-start(s32[1,512]{1,0:T(1,128)} %rows_marginal.3) | copy-start | bytes 6148
  3.9 11.3 %copy-start.2 = (s32[2,1,512,1,512]{4,3,2,1,0:T(1,128)S(1)}, s32[2,1,512,1,512]{4,3,2,1,0:T(1,128)}, u32[]{:S(2)}) copy-start(s32[2,1,512,1,512]{4,3,2,1,0:T(1,128)} %get-tuple-element.346) | copy-start | bytes 6291460 | tf_op jit(solution)/shard_map/cond
  4.8 36.2 %collective-permute-start.151 = (f32[512]{0:T(512)S(1)}, f32[512]{0:T(512)}, u32[]{:S(2)}, u32[]{:S(2)}) collective-permute-start(f32[512]{0:T(512)S(1)} %convert_log_fusion.1), channel_id=1, source_target_pairs={{0,2},{1,3},{2,0},{3,1},{4,6},{5,7},{6,4},{7,5},{8,10},{9,11},{10,... | collective-permute-start | bytes 6152 | tf_op jit(solution)/shard_map/cond/branch_1_fun/ppermute | solution.py:16
  4.8 10.7 %collective-permute-start.149 = (f32[1,128,256]{2,1,0:T(8,128)}, f32[1,128,256]{2,1,0:T(8,128)S(1)}, u32[]{:S(2)}, u32[]{:S(2)}) collective-permute-start(f32[1,128,256]{2,1,0:T(8,128)} %get-tuple-element.345), channel_id=1, source_target_pairs={{0,16},{8,24},{16,0},{24,8},{1,17},{9,25},{17,1},{25,9},{2,18},{10... | collective-permute-start | bytes 393224 | tf_op jit(solution)/shard_map/cond/branch_1_fun/ppermute | solution.py:16
  7.8 19.6 %collective-permute-start.148 = (f32[256,256]{1,0:T(8,128)S(1)}, f32[256,256]{1,0:T(8,128)}, u32[]{:S(2)}, u32[]{:S(2)}) collective-permute-start(f32[256,256]{1,0:T(8,128)S(1)} %get-tuple-element.643), channel_id=1, source_target_pairs={{0,2},{1,3},{2,0},{3,1},{4,6},{5,7},{6,4},{7,5},{8,10},{9,11},{10,... | collective-permute-start | bytes 786440 | tf_op jit(solution)/shard_map/cond/branch_1_fun/ppermute | solution.py:16
  9.4 31.6 %collective-permute-start.146 = (f32[512,256]{1,0:T(8,128)}, f32[512,256]{1,0:T(8,128)}, u32[]{:S(2)}, u32[]{:S(2)}) collective-permute-start(f32[512,256]{1,0:T(8,128)} %get-tuple-element.343), channel_id=1, source_target_pairs={{0,2},{1,3},{2,0},{3,1},{4,6},{5,7},{6,4},{7,5},{8,10},{9,11},{10,... | collective-permute-start | bytes 1572872 | tf_op jit(solution)/shard_map/cond/branch_1_fun/ppermute | solution.py:16
  11.7 29.3 %collective-permute-start.147 = (f32[512,256]{1,0:T(8,128)}, f32[512,256]{1,0:T(8,128)}, u32[]{:S(2)}, u32[]{:S(2)}) collective-permute-start(f32[512,256]{1,0:T(8,128)} %pad_maximum_fusion.2), channel_id=1, source_target_pairs={{0,5},{1,4},{2,7},{3,6},{4,1},{5,0},{6,3},{7,2},{8,13},{9,12},{10,... | collective-permute-start | bytes 1572872 | tf_op jit(solution)/shard_map/cond/branch_1_fun/ppermute | solution.py:16
  15.3 0.9 copy-start.6
  16.2 11.2 %collective-permute-start.150 = (f32[2,128,256]{2,1,0:T(8,128)S(1)}, f32[2,128,256]{2,1,0:T(8,128)S(1)}, u32[]{:S(2)}, u32[]{:S(2)}) collective-permute-start(f32[2,128,256]{2,1,0:T(8,128)S(1)} %maximum_bitcast_fusion.1), channel_id=1, source_target_pairs={{0,8},{8,0},{16,24},{24,16},{1,9},{9,1},{17,25},{25,17},{2,10},{10... | collective-permute-start | bytes 786440 | tf_op jit(solution)/shard_map/cond/branch_1_fun/ppermute | solution.py:16
  41.2 3.5 %copy-start.4 = (f32[1,128,256]{2,1,0:T(8,128)S(1)}, f32[1,128,256]{2,1,0:T(8,128)}, u32[]{:S(2)}) copy-start(f32[1,128,256]{2,1,0:T(8,128)} %param.36) | copy-start | bytes 393220
  41.3 3.5 %copy-start.32 = (f32[1,128,256]{2,1,0:T(8,128)S(1)}, f32[1,128,256]{2,1,0:T(8,128)}, u32[]{:S(2)}) copy-start(f32[1,128,256]{2,1,0:T(8,128)} %param.37) | copy-start | bytes 393220
  41.3 3.5 %copy-start.37 = (f32[1,1,512,256]{3,2,1,0:T(8,128)S(1)}, f32[1,1,512,256]{3,2,1,0:T(8,128)}, u32[]{:S(2)}) copy-start(f32[1,1,512,256]{3,2,1,0:T(8,128)} %param.40) | copy-start | bytes 1572868
  41.3 3.5 %copy-start.38 = (s32[1,1,512]{2,1,0:T(1,128)S(1)}, s32[1,1,512]{2,1,0:T(1,128)}, u32[]{:S(2)}) copy-start(s32[1,1,512]{2,1,0:T(1,128)} %param.41) | copy-start | bytes 6148
  41.3 3.5 %copy-start.39 = (f32[1,1,512,256]{3,2,1,0:T(8,128)S(1)}, f32[1,1,512,256]{3,2,1,0:T(8,128)}, u32[]{:S(2)}) copy-start(f32[1,1,512,256]{3,2,1,0:T(8,128)} %param.39) | copy-start | bytes 1572868
  44.9 1.6 %collective-permute-start.52 = (f32[2,128,256]{2,1,0:T(8,128)S(1)}, f32[2,128,256]{2,1,0:T(8,128)S(1)}, u32[]{:S(2)}, u32[]{:S(2)}) collective-permute-start(f32[2,128,256]{2,1,0:T(8,128)S(1)} %dynamic-slice_bitcast_fusion.1), channel_id=1, source_target_pairs={{0,8},{8,0},{16,24},{24,16},{1,9},{9,1},{17,25},{25,17},{2,10},{10... | collective-permute-start | bytes 786440 | tf_op jit(solution)/shard_map/cond/branch_1_fun/ppermute | solution.py:16
  46.5 5.6 %collective-permute-start.53 = (f32[1,128,256]{2,1,0:T(8,128)S(1)}, f32[1,128,256]{2,1,0:T(8,128)S(1)}, u32[]{:S(2)}, u32[]{:S(2)}) collective-permute-start(f32[1,128,256]{2,1,0:T(8,128)S(1)} %constant_dynamic-slice_fusion.1), channel_id=1, source_target_pairs={{0,16},{8,24},{16,0},{24,8},{1,17},{9,25},{17,1},{25,9},{2,18},{10... | collective-permute-start | bytes 393224 | tf_op jit(solution)/shard_map/cond/branch_1_fun/ppermute | solution.py:16
  48.3 24.6 %collective-permute-start.56 = (f32[512,256]{1,0:T(8,128)S(1)}, f32[512,256]{1,0:T(8,128)S(1)}, u32[]{:S(2)}, u32[]{:S(2)}) collective-permute-start(f32[512,256]{1,0:T(8,128)S(1)} %pad_maximum_fusion.21), channel_id=1, source_target_pairs={{0,7},{1,6},{2,5},{3,4},{4,3},{5,2},{6,1},{7,0},{8,15},{9,14},{10,... | collective-permute-start | bytes 1572872 | tf_op jit(solution)/shard_map/cond/branch_1_fun/ppermute | solution.py:16
  52.2 22.9 %copy-start.19 = (f32[128,256]{1,0:T(8,128)}, f32[128,256]{1,0:T(8,128)S(1)}, u32[]{:S(2)}) copy-start(f32[128,256]{1,0:T(8,128)S(1)} %get-tuple-element.899) | copy-start | bytes 393220 | tf_op jit(solution)/shard_map/cond
  52.2 5.0 %collective-permute-start.54 = (f32[1,128,256]{2,1,0:T(8,128)S(1)}, f32[1,128,256]{2,1,0:T(8,128)S(1)}, u32[]{:S(2)}, u32[]{:S(2)}) collective-permute-start(f32[1,128,256]{2,1,0:T(8,128)S(1)} %bitcast.816), channel_id=1, source_target_pairs={{0,16},{8,24},{16,0},{24,8},{1,17},{9,25},{17,1},{25,9},{2,18},{10... | collective-permute-start | bytes 393224 | tf_op jit(solution)/shard_map/cond/branch_1_fun/ppermute | solution.py:16
  52.8 23.2 %collective-permute-start.57 = (f32[512]{0:T(512)S(1)}, f32[512]{0:T(512)}, u32[]{:S(2)}, u32[]{:S(2)}) collective-permute-start(f32[512]{0:T(512)S(1)} %convert_log_fusion.14), channel_id=1, source_target_pairs={{0,5},{1,4},{2,7},{3,6},{4,1},{5,0},{6,3},{7,2},{8,13},{9,12},{10,... | collective-permute-start | bytes 6152 | tf_op jit(solution)/shard_map/cond/branch_1_fun/ppermute | solution.py:16
  57.3 17.8 %collective-permute-start.55 = (f32[2,128,256]{2,1,0:T(8,128)S(1)}, f32[2,128,256]{2,1,0:T(8,128)S(1)}, u32[]{:S(2)}, u32[]{:S(2)}) collective-permute-start(f32[2,128,256]{2,1,0:T(8,128)S(1)} %maximum_bitcast_fusion.14), channel_id=1, source_target_pairs={{0,8},{8,0},{16,24},{24,16},{1,9},{9,1},{17,25},{25,17},{2,10},{10... | collective-permute-start | bytes 786440 | tf_op jit(solution)/shard_map/cond/branch_1_fun/ppermute | solution.py:16
  76.0 3.7 %copy-start.31 = (f32[128,256]{1,0:T(8,128)S(1)}, f32[128,256]{1,0:T(8,128)}, u32[]{:S(2)}) copy-start(f32[128,256]{1,0:T(8,128)} %get-tuple-element.564) | copy-start | bytes 393220
  79.7 2.9 %collective-permute-start.158 = (f32[2,128,256]{2,1,0:T(8,128)S(1)}, f32[2,128,256]{2,1,0:T(8,128)S(1)}, u32[]{:S(2)}, u32[]{:S(2)}) collective-permute-start(f32[2,128,256]{2,1,0:T(8,128)S(1)} %dynamic-slice_bitcast_fusion.13), channel_id=1, source_target_pairs={{0,8},{8,0},{16,24},{24,16},{1,9},{9,1},{17,25},{25,17},{2,10},{10... | collective-permute-start | bytes 786440 | tf_op jit(solution)/shard_map/cond/branch_0_fun/ppermute | solution.py:16
  80.9 14.1 %collective-permute-start.160 = (f32[256,256]{1,0:T(8,128)S(1)}, f32[256,256]{1,0:T(8,128)S(1)}, u32[]{:S(2)}, u32[]{:S(2)}) collective-permute-start(f32[256,256]{1,0:T(8,128)S(1)} %get-tuple-element.718), channel_id=1, source_target_pairs={{0,7},{1,6},{2,5},{3,4},{4,3},{5,2},{6,1},{7,0},{8,15},{9,14},{10,... | collective-permute-start | bytes 786440 | tf_op jit(solution)/shard_map/cond/branch_0_fun/ppermute | solution.py:16
  82.7 13.5 %collective-permute-start.159 = (f32[1,128,256]{2,1,0:T(8,128)S(1)}, f32[1,128,256]{2,1,0:T(8,128)S(1)}, u32[]{:S(2)}, u32[]{:S(2)}) collective-permute-start(f32[1,128,256]{2,1,0:T(8,128)S(1)} %constant_dynamic-slice_fusion.13), channel_id=1, source_target_pairs={{0,16},{8,24},{16,0},{24,8},{1,17},{9,25},{17,1},{25,9},{2,18},{10... | collective-permute-start | bytes 393224 | tf_op jit(solution)/shard_map/cond/branch_0_fun/ppermute | solution.py:16
  96.1 0.9 copy-start.35
  96.1 1.0 %copy-start.33 = (f32[512,256]{1,0:T(8,128)}, f32[512,256]{1,0:T(8,128)S(1)}, u32[]{:S(2)}) copy-start(f32[512,256]{1,0:T(8,128)S(1)} %branch_0_fun.14) | copy-start | bytes 1572868 | tf_op jit(solution)/shard_map/cond
where the time goes:
time: 98.3 us; the launch traced here: 97.2 us
  waiting for transfers between devices  58.2 us (59%)
  starting transfers between devices  12.7 us (13%)
  local copies, waits for them, and re-layouts  8.5 us (9%)
  other arithmetic  7.36 us (7%)
  Pallas kernels  7.12 us (7%)
  between operations  2.7 us (3%)
    ppermute x15, waiting for transfers between devices, move(): return lax.ppermute(value, axis, pairs)  58.2 us
    ppermute x15, starting transfers between devices, move(): return lax.ppermute(value, axis, pairs)  12.7 us
    pallas_call x2, Pallas kernels, tile_grads(): pl.pallas_call(tile_kernel, out_shape=[jax.ShapeDtypeStruct(held.shape, j...  7.11 us
    sub x3, other arithmetic, adagrad(): return (param - learn_rate * grad / jnp.sqrt(accum), accum)  2.26 us
  transfers between devices with their start and end apart: 15, of which 7 were waited for; matrix products, arithmetic and copies ran while one was open for 12% of the time, Pallas kernels for 0%

commit v1 on v0

--- a/solution.py
+++ b/solution.py
@@ -37,11 +37,19 @@
     return blocks[0]
 
 
-def row_gather(value):
+def row_gather(value, beyond=None):
     size = lax.axis_size("row")
     if size & (size - 1):
         return lax.all_gather(value, "row", axis=0, tiled=True)
     me = lax.axis_index("row")
+    if size == 4:
+        beyond = move(value, "row", 2) if beyond is None else beyond
+        blocks = jnp.stack([value, move(value, "row", 1), beyond, move(beyond, "row", 1)])
+        for bit in range(2):
+            pairs = blocks.reshape(-1, 2, 1 << bit, *value.shape)
+            pairs = jnp.where((me >> bit) & 1 == 0, pairs, pairs[:, ::-1])
+            blocks = pairs.reshape(blocks.shape)
+        return blocks.reshape(-1, value.shape[1])
     blocks = value[None]
     for bit in reversed(range(size.bit_length() - 1)):
         other = move(blocks, "row", 1 << bit)
@@ -129,13 +137,15 @@
     return jnp.log(marginals.astype(jnp.float32))
 
 
-def direct_first(first, second):
+def early_masks(first, second):
+    both = first ^ second
     if not (crosses(first) and crosses(second)):
-        return 0
-    both = first ^ second
+        return 0, 0
     if both & 1 == 0:
-        return 1
-    return 0 if first & 1 else 2
+        return both, 0
+    if first & 1:
+        return both & ~1, 0
+    return both, both
 
 
 def before(first, second, state):
@@ -144,38 +154,39 @@
     held = first_of_all(move(cols, "col", first))
     both = first ^ second
     half = tile_cols // 2
-    early = direct_first(first, second)
+    acc_by, cols_by = early_masks(first, second)
     last, next_acc, waiting = unused(cols), unused(acc), unused(acc[half:])
     if not crosses(first):
         last = move(jnp.concatenate([cols[:half], acc[:half]]), "col", both)
         last = first_of_all(last, 5)
         waiting = first_of_all(move(acc[half:], "col", first), 5)
-    if early > 0:
-        next_acc = first_of_all(move(acc, "col", both), 5)
-    if early > 1:
-        last = first_of_all(move(cols, "col", both), 5)
-    log_now = move(log_of(cols_marginal), "col", first)
-    whole = row_gather(shard)
+    if acc_by:
+        next_acc = first_of_all(move(acc, "col", acc_by), 5)
+    if cols_by:
+        last = first_of_all(move(cols, "col", cols_by), 5)
+    beyond, cols_marginal = lax.optimization_barrier((move(shard, "row", 2), cols_marginal))
+    whole = row_gather(shard, beyond)
+    log_cols = log_of(cols_marginal)
+    log_now, log_next = move(log_cols, "col", first), move(log_cols, "col", both)
     tiles = lax.optimization_barrier(
         [counts[t].reshape(rows_block, tile_cols) for t in range(rounds)]
     )
-    return held, last, next_acc, waiting, log_now, whole, tiles
+    return held, last, next_acc, waiting, log_now, log_next, whole, tiles
 
 
 def between(first, second, state):
-    shard, shard_acc, cols, acc, cols_marginal, held, last, next_acc, waiting = state[:9]
-    grad, grad_rows = state[9:]
+    shard, shard_acc, cols, acc, held, last, next_acc, waiting, grad, grad_rows = state
     both = first ^ second
     half = cols.shape[0] // 2
     if crosses(first):
-        early = direct_first(first, second)
+        acc_by, cols_by = early_masks(first, second)
+        if acc_by != both:
+            next_acc = move(next_acc if acc_by else acc, "col", both ^ acc_by)
         grad = move(grad, "col", second)
         if not crosses(second):
             last = move(held, "col", second)
-        elif early < 2:
+        elif cols_by != both:
             last = move(cols, "col", both)
-        if early < 1:
-            next_acc = move(acc, "col", both)
         last, next_acc = adagrad(last, next_acc, grad)
     else:
         later, later_acc = adagrad(held[half:], waiting, grad[half:])
@@ -184,9 +195,8 @@
         last = jnp.concatenate([front, sent[half:]])
         next_acc = jnp.concatenate([front_acc, later_acc])
     last, next_acc = first_of_all(last), first_of_all(next_acc)
-    log_next = move(log_of(cols_marginal), "col", both)
     shard, shard_acc = adagrad(shard, shard_acc, row_sum_scatter(grad_rows))
-    return shard, shard_acc, row_gather(shard), last, next_acc, log_next
+    return shard, shard_acc, row_gather(shard), last, next_acc
 
 
 def after(late, state):
@@ -213,15 +223,15 @@
     def by_plan(step, state):
         return lax.switch(which, [lambda s, a=a, b=b: step(a, b, s) for a, b in pairs], state)
 
-    held, last, next_acc, waiting, log_now, whole, tiles = by_plan(
+    held, last, next_acc, waiting, log_now, log_next, whole, tiles = by_plan(
         before, (shard, cols, acc, cols_marginal, counts)
     )
     grad, grad_rows = tile_grads(tiles[0], whole, held, rows_marginal, log_now)
-    shard, shard_acc, whole, held, held_acc, log_next = by_plan(
+    shard, shard_acc, whole, held, held_acc = by_plan(
         between,
         (
-            *(shard, shard_acc, cols, acc, cols_marginal),
-            *(held, last, next_acc, waiting, grad, grad_rows),
+            *(shard, shard_acc, cols, acc, held),
+            *(last, next_acc, waiting, grad, grad_rows),
         ),
     )
     grad, grad_rows = tile_grads(tiles[1], whole, held, rows_marginal, log_next)

time: 98.3 us -> 77.5 us (0.79)
  waiting for transfers between devices: 58.2 us -> 45 us
  local copies, waits for them, and re-layouts: 8.5 us -> 4.53 us
  other arithmetic: 7.36 us -> 5.43 us
    ppermute x15 -> x16, waiting for transfers between devices: 58.2 us -> 45 us  [move(): return lax.ppermute(value, axis, pairs)]
    slice x3 -> x0, local copies, waits for them, and re-layouts: 3.13 us -> none  [the longest x1 1.07 us: after(): held_acc = jnp.concatenate([held_acc[:half], moved])]
    concatenate x3 -> x0, other arithmetic: 1.97 us -> none  [the longest x1 1.1 us: between(): last = jnp.concatenate([front, sent[half:]])]
    sub x3, other arithmetic: 2.26 us -> 3.59 us  [adagrad(): return (param - learn_rate * grad / jnp.sqrt(accum), accum)]
    add x1 -> x0, other arithmetic: 1.16 us -> none  [adagrad(): accum = accum + grad * grad]
    squeeze x1, local copies, waits for them, and re-layouts: 1.19 us -> 0.17 us  [before(): counts[t].reshape(rows_block, tile_cols)]
    unnamed x14, local copies, waits for them, and re-layouts: 0.04 us -> 1.03 us
    ppermute x15 -> x16, starting transfers between devices: 12.7 us -> 12 us  [move(): return lax.ppermute(value, axis, pairs)]
  transfers between devices with their start and end apart: 15 -> 16, of which waited for: 7 -> 8; matrix products, arithmetic and copies ran while one was open for 12% -> 8% of each run, Pallas kernels for 0% -> 0%
where the time goes in v1:
time: 77.5 us; the launch traced here: 77.2 us
  waiting for transfers between devices  45 us (58%)
  starting transfers between devices  12 us (15%)
  Pallas kernels  6.99 us (9%)
  other arithmetic  5.43 us (7%)
  local copies, waits for them, and re-layouts  4.53 us (6%)
  between operations  2.66 us (3%)
    ppermute x16, waiting for transfers between devices, move(): return lax.ppermute(value, axis, pairs)  45 us
    ppermute x16, starting transfers between devices, move(): return lax.ppermute(value, axis, pairs)  12 us
    pallas_call x2, Pallas kernels, tile_grads(): pl.pallas_call(tile_kernel, out_shape=[jax.ShapeDtypeStruct(held.shape, j...  6.98 us
    sub x3, other arithmetic, adagrad(): return (param - learn_rate * grad / jnp.sqrt(accum), accum)  3.59 us
    another operation x1, local copies, waits for them, and re-layouts  1.76 us
  transfers between devices with their start and end apart: 16, of which 8 were waited for; matrix products, arithmetic and copies ran while one was open for 8% of the time, Pallas kernels for 0%

profile of v1, /device:TPU:8, one launch (start us, length us, event | category | flops | bytes accessed | tf_op | source)
XLA Modules:
  0.0 77.2 jit_solution(16486804977253086945)
XLA Ops:
  0.6 1.3 %fusion.49 = (s32[1]{0:T(128)}, s32[1]{0:T(128)}) fusion(s32[2]{0:T(128)} %param.43), kind=kLoop, calls=%fused_computation.304 | loop fusion | bytes 16 | tf_op jit(solution)/shard_map/slice | solution.py:221
  3.9 0.0 copy-start
  3.9 28.6 %conditional.3 = (f32[512,256]{1,0:T(8,128)}, f32[512,256]{1,0:T(8,128)}, f32[512,256]{1,0:T(8,128)}, f32[256,256]{1,0:T(8,128)}, f32[512,256]{1,0:T(8,128)}, /*...) conditional(s32[]{:T(128)} %bitcast.305, ...), branch_computations={%region_0.1_spmd, %region_1.2_spmd, %region_2.3_spmd, %region_3.4_... | conditional | flops 786953 | bytes 829913280 | solution.py:224
  4.0 1.6 %collective-permute-start.63 = (f32[128,256]{1,0:T(8,128)}, f32[128,256]{1,0:T(8,128)S(1)}, u32[]{:S(2)}, u32[]{:S(2)}) collective-permute-start(f32[128,256]{1,0:T(8,128)} %bitcast.618), channel_id=1, source_target_pairs={{0,16},{8,24},{16,0},{24,8},{1,17},{9,25},{17,1},{25,9},{2,18},{10... | collective-permute-start | bytes 393224 | tf_op jit(solution)/shard_map/cond/branch_12_fun/ppermute | solution.py:16
  5.5 0.0 collective-permute-start.62
  5.5 2.5 %collective-permute-start.61 = (f32[512,256]{1,0:T(8,128)}, f32[512,256]{1,0:T(8,128)}, u32[]{:S(2)}, u32[]{:S(2)}) collective-permute-start(f32[512,256]{1,0:T(8,128)} %get-tuple-element.454), channel_id=1, source_target_pairs={{0,7},{1,6},{2,5},{3,4},{4,3},{5,2},{6,1},{7,0},{8,15},{9,14},{10,... | collective-permute-start | bytes 1572872 | tf_op jit(solution)/shard_map/cond/branch_12_fun/ppermute | solution.py:16
  8.1 1.8 %copy.100 = s32[2,1,512,1,512]{4,2,3,1,0:T(8,128)S(1)} copy(s32[2,1,512,1,512]{4,3,2,1,0:T(1,128)} %get-tuple-element.459) | data formatting | bytes 4194304 | tf_op jit(solution)/shard_map
  9.8 0.0 copy-start.52
  9.8 0.0 copy-start.17
  9.8 0.2 slice_bitcast_fusion.24
  10.1 0.0 collective-permute-done.63
  10.1 0.3 collective-permute-start.64
  10.4 0.1 copy-done.52
  10.5 0.6 collective-permute-start.66
  11.1 1.4 %collective-permute-start.65 = (f32[512]{0:T(512)S(1)}, f32[512]{0:T(512)}, u32[]{:S(2)}, u32[]{:S(2)}) collective-permute-start(f32[512]{0:T(512)S(1)} %convert_log_fusion.12), channel_id=1, source_target_pairs={{0,7},{1,6},{2,5},{3,4},{4,3},{5,2},{6,1},{7,0},{8,15},{9,14},{10,... | collective-permute-start | bytes 6152 | tf_op jit(solution)/shard_map/cond/branch_12_fun/ppermute | solution.py:16
  12.5 0.0 collective-permute-done.62
  12.5 0.0 collective-permute-done.64
  12.5 0.0 copy-done.17
  12.6 0.8 %reverse_select_fusion.24 = f32[1,2,2,128,256]{4,3,2,1,0:T(8,128)} fusion(f32[1,2,2,128,256]{4,3,2,1,0:T(8,128)S(1)} %fusion.12, pred[]{:T(512)S(6)} %eq.128), kind=kLoop, calls=%fused_computation.89 | loop fusion | flops 131072 | bytes 1048577 | tf_op jit(solution)/shard_map/cond/branch_12_fun/jit(_where)/select_n | solution.py:50
  13.5 19.0 %collective-permute-done.61.source = f32[512,256]{1,0:T(8,128)} collective-permute-done((f32[512,256]{1,0:T(8,128)}, f32[512,256]{1,0:T(8,128)}, u32[]{:S(2)}, u32[]{:S(2)}) %collective-permute-start.61) | collective-permute-done | bytes 524320 | tf_op jit(solution)/shard_map/cond/branch_12_fun/ppermute | solution.py:16
  32.4 0.1 collective-permute-done.66
  32.5 0.0 collective-permute-done.65
  32.5 1.0 %copy-done.39 = s32[512,512]{1,0:T(8,128)} copy-done((s32[512,512]{1,0:T(8,128)}, s32[512,512]{1,0:T(8,128)S(1)}, u32[]{:S(2)}) %copy-start.39) | copy-done | bytes 1048600
  33.5 0.0 copy-done
  33.5 0.0 copy-start.38
  33.6 3.4 %shard_map.119 = (f32[512,256]{1,0:T(8,128)S(1)}, f32[512,256]{1,0:T(8,128)S(1)}) custom-call(s32[512,512]{1,0:T(8,128)S(1)} %get-tuple-element.579.tile, f32[512,256]{1,0:T(8,128)} %get-tuple-element.580.whole, f32[512,256]{1,0:T(8,128)} %get-tuple-element.581.held, s32[1,512]{1,0:T(1,128)S(1)} %copy-done, f32[1,512]{1,0:T(1,128)} %get-tuple-element.582.log_c), custom_call_target="tpu_custom_call" | custom-call | flops 1207959552 | bytes 3145728 | tf_op jit(solution)/shard_map/pallas_call | solution.py:117
  37.0 0.0 copy-done.4
  37.0 0.0 copy-done.32
  37.0 0.0 copy-done.37
  37.0 0.0 copy-done.38
  37.0 28.5 %conditional.4 = (f32[128,256]{1,0:T(8,128)}, f32[128,256]{1,0:T(8,128)S(1)}, f32[512,256]{1,0:T(8,128)S(1)}, f32[512,256]{1,0:T(8,128)}, f32[512,256]{1,0:T(8,128)}) conditional(s32[]{:T(128)} %bitcast.305, (f32[512,256]{1,0:T(8,128)S(1)}, f32[128,256]{1,0:T(8,128)S(1)}, f32[128,256]{1,0:T(8,128)S(1)}, ...), branch_computations={%region_13.14_spmd, %region_14.15_spmd, %region_15.16_spmd, %regio... | conditional | flops 1966103 | bytes 818088640 | solution.py:224
  37.1 0.1 collective-permute-start.151
  37.2 1.5 %collective-permute-start.156 = (f32[512,256]{1,0:T(8,128)}, f32[512,256]{1,0:T(8,128)S(1)}, u32[]{:S(2)}, u32[]{:S(2)}) collective-permute-start(f32[512,256]{1,0:T(8,128)} %get-tuple-element.541), channel_id=1, source_target_pairs={{0,1},{1,0},{2,3},{3,2},{4,5},{5,4},{6,7},{7,6},{8,9},{9,8},{10,11... | collective-permute-start | bytes 1572872 | tf_op jit(solution)/shard_map/cond/branch_12_fun/ppermute | solution.py:16
  38.8 0.5 collective-permute-start.157
  39.3 1.6 %collective-permute-start.158 = (f32[512,256]{1,0:T(8,128)S(1)}, f32[512,256]{1,0:T(8,128)}, u32[]{:S(2)}, u32[]{:S(2)}) collective-permute-start(f32[512,256]{1,0:T(8,128)S(1)} %get-tuple-element.543), channel_id=1, source_target_pairs={{0,6},{1,7},{2,4},{3,5},{4,2},{5,3},{6,0},{7,1},{8,14},{9,15},{10,... | collective-permute-start | bytes 1572872 | tf_op jit(solution)/shard_map/cond/branch_12_fun/ppermute | solution.py:16
  40.9 0.0 collective-permute-done.151
  40.9 0.6 collective-permute-start.152
  41.5 4.5 %collective-permute-done.152 = f32[1,128,256]{2,1,0:T(8,128)S(1)} collective-permute-done((f32[1,128,256]{2,1,0:T(8,128)S(1)}, f32[1,128,256]{2,1,0:T(8,128)S(1)}, u32[]{:S(2)}, u32[]{:S(2)}) %collective-permute-start.152) | collective-permute-done | bytes 131104 | tf_op jit(solution)/shard_map/cond/branch_12_fun/ppermute | solution.py:16
  46.1 0.0 copy-start.30
  46.1 0.6 collective-permute-start.154
  46.7 0.0 collective-permute-start.153
  46.7 4.4 %collective-permute-done.154 = f32[128,256]{1,0:T(8,128)S(1)} collective-permute-done((f32[128,256]{1,0:T(8,128)S(1)}, f32[128,256]{1,0:T(8,128)S(1)}, u32[]{:S(2)}, u32[]{:S(2)}) %collective-permute-start.154) | collective-permute-done | bytes 131104 | tf_op jit(solution)/shard_map/cond/branch_12_fun/ppermute | solution.py:16
  51.1 0.0 collective-permute-start.155
  51.1 1.1 %collective-permute-done.156 = f32[512,256]{1,0:T(8,128)S(1)} collective-permute-done((f32[512,256]{1,0:T(8,128)}, f32[512,256]{1,0:T(8,128)S(1)}, u32[]{:S(2)}, u32[]{:S(2)}) %collective-permute-start.156) | collective-permute-done | bytes 524320 | tf_op jit(solution)/shard_map/cond/branch_12_fun/ppermute | solution.py:16
  52.2 10.8 %collective-permute-done.157 = f32[512,256]{1,0:T(8,128)S(1)} collective-permute-done((f32[512,256]{1,0:T(8,128)S(1)}, f32[512,256]{1,0:T(8,128)S(1)}, u32[]{:S(2)}, u32[]{:S(2)}) %collective-permute-start.157) | collective-permute-done | bytes 524320 | tf_op jit(solution)/shard_map/cond/branch_12_fun/ppermute | solution.py:16
  63.0 0.0 collective-permute-done.158
  63.0 2.2 %multiply_subtract_fusion.15 = (f32[512,256]{1,0:T(8,128)}, f32[512,256]{1,0:T(8,128)}) fusion(f32[512,256]{1,0:T(8,128)S(1)} %collective-permute-done.156, f32[512,256]{1,0:T(8,128)S(1)} %collective-permute-done.157, f32[512,256]{1,0:T(8,128)} %collective-permute-done.158), kind=kLoop, calls=%fused_computation.269 | loop fusion | flops 655360 | bytes 2621440 | tf_op jit(solution)/shard_map/cond/branch_12_fun/sub | solution.py:21
  65.2 0.0 collective-permute-done.153
  65.2 0.0 collective-permute-done.155
  65.2 0.0 copy-done.30
  65.6 0.0 copy-start.31
  65.6 3.5 %shard_map.120 = (f32[512,256]{1,0:T(8,128)S(1)}, f32[512,256]{1,0:T(8,128)S(1)}) custom-call(s32[512,512]{1,0:T(8,128)} %copy-done.39, f32[512,256]{1,0:T(8,128)S(1)} %get-tuple-element.588.whole, f32[512,256]{1,0:T(8,128)} %get-tuple-element.589.held, s32[1,512]{1,0:T(1,128)S(1)} %copy-done, f32[1,512]{1,0:T(1,128)} %get-tuple-element.590.log_c), custom_call_target="tpu_custom_call" | custom-call | flops 1207959552 | bytes 3145728 | tf_op jit(solution)/shard_map/pallas_call | solution.py:117
  69.1 0.0 copy-done.31
  69.2 8.1 %conditional.5 = (f32[1,128,256]{2,1,0:T(8,128)}, f32[1,128,256]{2,1,0:T(8,128)}, f32[1,1,512,256]{3,2,1,0:T(8,128)}, f32[1,1,512,256]{3,2,1,0:T(8,128)}) conditional(s32[]{:T(128)} %bitcast.304, (f32[512,256]{1,0:T(8,128)S(1)}, f32[128,256]{1,0:T(8,128)S(1)}, f32[128,256]{1,0:T(8,128)S(1)}, f32[512,256]{1,0:T(8,128)S(1)}, f32[512,256]{1,0:T(8,128)}, ...), branch_computations={%region_26.27_spmd, %region_27.28_spmd} | conditional | flops 1048597 | bytes 812845440 | solution.py:238
  69.2 0.1 collective-permute-start.159
  69.3 1.5 %collective-permute-done.159 = f32[2,128,256]{2,1,0:T(8,128)S(1)} collective-permute-done((f32[2,128,256]{2,1,0:T(8,128)S(1)}, f32[2,128,256]{2,1,0:T(8,128)S(1)}, u32[]{:S(2)}, u32[]{:S(2)}) %collective-permute-start.159) | collective-permute-done | bytes 262176 | tf_op jit(solution)/shard_map/cond/branch_1_fun/ppermute | solution.py:16
  70.9 0.6 collective-permute-start.160
  71.5 1.3 %multiply_subtract_fusion.17 = (f32[512,256]{1,0:T(8,128)S(1)}, f32[512,256]{1,0:T(8,128)S(1)}) fusion(f32[512,256]{1,0:T(8,128)} %get-tuple-element.553, f32[512,256]{1,0:T(8,128)S(1)} %get-tuple-element.554, f32[512,256]{1,0:T(8,128)} %get-tuple-element.555), kind=kLoop, calls=%fused_computation.289 | loop fusion | flops 655360 | bytes 2621440 | tf_op jit(solution)/shard_map/cond/branch_1_fun/sub | solution.py:21
  72.8 0.0 copy-start.34
  72.9 0.0 copy-start.36
  72.9 3.6 %collective-permute-done.160 = f32[1,128,256]{2,1,0:T(8,128)S(1)} collective-permute-done((f32[1,128,256]{2,1,0:T(8,128)S(1)}, f32[1,128,256]{2,1,0:T(8,128)S(1)}, u32[]{:S(2)}, u32[]{:S(2)}) %collective-permute-start.160) | collective-permute-done | bytes 131104 | tf_op jit(solution)/shard_map/cond/branch_1_fun/ppermute | solution.py:16
  76.5 0.7 fusion.44
  77.2 0.0 copy-done.34
  77.2 0.0 copy-done.36
  (25 shorter events, 0.4 us)
Async XLA Ops:
  3.9 29.6 %copy-start = (s32[1,512]{1,0:T(1,128)S(1)}, s32[1,512]{1,0:T(1,128)}, u32[]{:S(2)}) copy-start(s32[1,512]{1,0:T(1,128)} %rows_marginal.3) | copy-start | bytes 6148
  4.0 6.1 %collective-permute-start.63 = (f32[128,256]{1,0:T(8,128)}, f32[128,256]{1,0:T(8,128)S(1)}, u32[]{:S(2)}, u32[]{:S(2)}) collective-permute-start(f32[128,256]{1,0:T(8,128)} %bitcast.618), channel_id=1, source_target_pairs={{0,16},{8,24},{16,0},{24,8},{1,17},{9,25},{17,1},{25,9},{2,18},{10... | collective-permute-start | bytes 393224 | tf_op jit(solution)/shard_map/cond/branch_12_fun/ppermute | solution.py:16
  5.5 7.0 %collective-permute-start.62 = (f32[128,256]{1,0:T(8,128)}, f32[128,256]{1,0:T(8,128)S(1)}, u32[]{:S(2)}, u32[]{:S(2)}) collective-permute-start(f32[128,256]{1,0:T(8,128)} %bitcast.619), channel_id=1, source_target_pairs={{0,8},{8,0},{16,24},{24,16},{1,9},{9,1},{17,25},{25,17},{2,10},{10... | collective-permute-start | bytes 393224 | tf_op jit(solution)/shard_map/cond/branch_12_fun/ppermute | solution.py:16
  5.5 26.9 %collective-permute-start.61 = (f32[512,256]{1,0:T(8,128)}, f32[512,256]{1,0:T(8,128)}, u32[]{:S(2)}, u32[]{:S(2)}) collective-permute-start(f32[512,256]{1,0:T(8,128)} %get-tuple-element.454), channel_id=1, source_target_pairs={{0,7},{1,6},{2,5},{3,4},{4,3},{5,2},{6,1},{7,0},{8,15},{9,14},{10,... | collective-permute-start | bytes 1572872 | tf_op jit(solution)/shard_map/cond/branch_12_fun/ppermute | solution.py:16
  9.8 0.7 copy-start.52
  9.8 2.7 %copy-start.17 = (f32[1,128,256]{2,1,0:T(8,128)S(1)}, f32[1,128,256]{2,1,0:T(8,128)}, u32[]{:S(2)}) copy-start(f32[1,128,256]{2,1,0:T(8,128)} %get-tuple-element.455) | copy-start | bytes 393220 | tf_op jit(solution)/shard_map/cond
  10.1 2.5 %collective-permute-start.64 = (f32[128,256]{1,0:T(8,128)S(1)}, f32[128,256]{1,0:T(8,128)S(1)}, u32[]{:S(2)}, u32[]{:S(2)}) collective-permute-start(f32[128,256]{1,0:T(8,128)S(1)} %collective-permute-done.63), channel_id=1, source_target_pairs={{0,8},{8,0},{16,24},{24,16},{1,9},{9,1},{17,25},{25,17},{2,10},{10... | collective-permute-start | bytes 393224 | tf_op jit(solution)/shard_map/cond/branch_12_fun/ppermute | solution.py:16
  10.5 22.0 %collective-permute-start.66 = (f32[512]{0:T(512)S(1)}, f32[512]{0:T(512)}, u32[]{:S(2)}, u32[]{:S(2)}) collective-permute-start(f32[512]{0:T(512)S(1)} %convert_log_fusion.12), channel_id=1, source_target_pairs={{0,6},{1,7},{2,4},{3,5},{4,2},{5,3},{6,0},{7,1},{8,14},{9,15},{10,... | collective-permute-start | bytes 6152 | tf_op jit(solution)/shard_map/cond/branch_12_fun/ppermute | solution.py:16
  11.1 21.4 %collective-permute-start.65 = (f32[512]{0:T(512)S(1)}, f32[512]{0:T(512)}, u32[]{:S(2)}, u32[]{:S(2)}) collective-permute-start(f32[512]{0:T(512)S(1)} %convert_log_fusion.12), channel_id=1, source_target_pairs={{0,7},{1,6},{2,5},{3,4},{4,3},{5,2},{6,1},{7,0},{8,15},{9,14},{10,... | collective-permute-start | bytes 6152 | tf_op jit(solution)/shard_map/cond/branch_12_fun/ppermute | solution.py:16
  32.5 1.0 %copy-start.39 = (s32[512,512]{1,0:T(8,128)}, s32[512,512]{1,0:T(8,128)S(1)}, u32[]{:S(2)}) copy-start(s32[512,512]{1,0:T(8,128)S(1)} %get-tuple-element.578.tile) | copy-start | bytes 3145732
  33.5 3.5 %copy-start.4 = (f32[1,128,256]{2,1,0:T(8,128)S(1)}, f32[1,128,256]{2,1,0:T(8,128)}, u32[]{:S(2)}) copy-start(f32[1,128,256]{2,1,0:T(8,128)} %param.36) | copy-start | bytes 393220
  33.5 3.5 %copy-start.32 = (f32[1,128,256]{2,1,0:T(8,128)S(1)}, f32[1,128,256]{2,1,0:T(8,128)}, u32[]{:S(2)}) copy-start(f32[1,128,256]{2,1,0:T(8,128)} %param.37) | copy-start | bytes 393220
  33.5 3.5 %copy-start.37 = (f32[1,1,512,256]{3,2,1,0:T(8,128)S(1)}, f32[1,1,512,256]{3,2,1,0:T(8,128)}, u32[]{:S(2)}) copy-start(f32[1,1,512,256]{3,2,1,0:T(8,128)} %param.40) | copy-start | bytes 1572868
  33.5 3.5 %copy-start.38 = (f32[1,1,512,256]{3,2,1,0:T(8,128)S(1)}, f32[1,1,512,256]{3,2,1,0:T(8,128)}, u32[]{:S(2)}) copy-start(f32[1,1,512,256]{3,2,1,0:T(8,128)} %param.39) | copy-start | bytes 1572868
  37.1 3.8 %collective-permute-start.151 = (f32[2,128,256]{2,1,0:T(8,128)S(1)}, f32[2,128,256]{2,1,0:T(8,128)S(1)}, u32[]{:S(2)}, u32[]{:S(2)}) collective-permute-start(f32[2,128,256]{2,1,0:T(8,128)S(1)} %dynamic-slice_bitcast_fusion.12), channel_id=1, source_target_pairs={{0,8},{8,0},{16,24},{24,16},{1,9},{9,1},{17,25},{25,17},{2,10},{10... | collective-permute-start | bytes 786440 | tf_op jit(solution)/shard_map/cond/branch_12_fun/ppermute | solution.py:16
  37.2 15.0 %collective-permute-start.156 = (f32[512,256]{1,0:T(8,128)}, f32[512,256]{1,0:T(8,128)S(1)}, u32[]{:S(2)}, u32[]{:S(2)}) collective-permute-start(f32[512,256]{1,0:T(8,128)} %get-tuple-element.541), channel_id=1, source_target_pairs={{0,1},{1,0},{2,3},{3,2},{4,5},{5,4},{6,7},{7,6},{8,9},{9,8},{10,11... | collective-permute-start | bytes 1572872 | tf_op jit(solution)/shard_map/cond/branch_12_fun/ppermute | solution.py:16
  38.8 24.2 %collective-permute-start.157 = (f32[512,256]{1,0:T(8,128)S(1)}, f32[512,256]{1,0:T(8,128)S(1)}, u32[]{:S(2)}, u32[]{:S(2)}) collective-permute-start(f32[512,256]{1,0:T(8,128)S(1)} %get-tuple-element.542), channel_id=1, source_target_pairs={{0,1},{1,0},{2,3},{3,2},{4,5},{5,4},{6,7},{7,6},{8,9},{9,8},{10,11... | collective-permute-start | bytes 1572872 | tf_op jit(solution)/shard_map/cond/branch_12_fun/ppermute | solution.py:16
  39.3 23.7 %collective-permute-start.158 = (f32[512,256]{1,0:T(8,128)S(1)}, f32[512,256]{1,0:T(8,128)}, u32[]{:S(2)}, u32[]{:S(2)}) collective-permute-start(f32[512,256]{1,0:T(8,128)S(1)} %get-tuple-element.543), channel_id=1, source_target_pairs={{0,6},{1,7},{2,4},{3,5},{4,2},{5,3},{6,0},{7,1},{8,14},{9,15},{10,... | collective-permute-start | bytes 1572872 | tf_op jit(solution)/shard_map/cond/branch_12_fun/ppermute | solution.py:16
  40.9 5.1 %collective-permute-start.152 = (f32[1,128,256]{2,1,0:T(8,128)S(1)}, f32[1,128,256]{2,1,0:T(8,128)S(1)}, u32[]{:S(2)}, u32[]{:S(2)}) collective-permute-start(f32[1,128,256]{2,1,0:T(8,128)S(1)} %constant_dynamic-slice_fusion.12), channel_id=1, source_target_pairs={{0,16},{8,24},{16,0},{24,8},{1,17},{9,25},{17,1},{25,9},{2,18},{10... | collective-permute-start | bytes 393224 | tf_op jit(solution)/shard_map/cond/branch_12_fun/ppermute | solution.py:16
  46.1 19.1 %copy-start.30 = (f32[128,256]{1,0:T(8,128)}, f32[128,256]{1,0:T(8,128)S(1)}, u32[]{:S(2)}) copy-start(f32[128,256]{1,0:T(8,128)S(1)} %get-tuple-element.891) | copy-start | bytes 393220 | tf_op jit(solution)/shard_map/cond
  46.1 5.0 %collective-permute-start.154 = (f32[128,256]{1,0:T(8,128)S(1)}, f32[128,256]{1,0:T(8,128)S(1)}, u32[]{:S(2)}, u32[]{:S(2)}) collective-permute-start(f32[128,256]{1,0:T(8,128)S(1)} %get-tuple-element.891), channel_id=1, source_target_pairs={{0,16},{8,24},{16,0},{24,8},{1,17},{9,25},{17,1},{25,9},{2,18},{10... | collective-permute-start | bytes 393224 | tf_op jit(solution)/shard_map/cond/branch_12_fun/ppermute | solution.py:16
  46.7 18.5 %collective-permute-start.153 = (f32[128,256]{1,0:T(8,128)S(1)}, f32[128,256]{1,0:T(8,128)S(1)}, u32[]{:S(2)}, u32[]{:S(2)}) collective-permute-start(f32[128,256]{1,0:T(8,128)S(1)} %get-tuple-element.891), channel_id=1, source_target_pairs={{0,8},{8,0},{16,24},{24,16},{1,9},{9,1},{17,25},{25,17},{2,10},{10... | collective-permute-start | bytes 393224 | tf_op jit(solution)/shard_map/cond/branch_12_fun/ppermute | solution.py:16
  51.1 14.1 %collective-permute-start.155 = (f32[128,256]{1,0:T(8,128)S(1)}, f32[128,256]{1,0:T(8,128)S(1)}, u32[]{:S(2)}, u32[]{:S(2)}) collective-permute-start(f32[128,256]{1,0:T(8,128)S(1)} %collective-permute-done.154), channel_id=1, source_target_pairs={{0,8},{8,0},{16,24},{24,16},{1,9},{9,1},{17,25},{25,17},{2,10},{10... | collective-permute-start | bytes 393224 | tf_op jit(solution)/shard_map/cond/branch_12_fun/ppermute | solution.py:16
  65.6 3.6 %copy-start.31 = (f32[128,256]{1,0:T(8,128)S(1)}, f32[128,256]{1,0:T(8,128)}, u32[]{:S(2)}) copy-start(f32[128,256]{1,0:T(8,128)} %get-tuple-element.593) | copy-start | bytes 393220
  69.2 1.6 %collective-permute-start.159 = (f32[2,128,256]{2,1,0:T(8,128)S(1)}, f32[2,128,256]{2,1,0:T(8,128)S(1)}, u32[]{:S(2)}, u32[]{:S(2)}) collective-permute-start(f32[2,128,256]{2,1,0:T(8,128)S(1)} %dynamic-slice_bitcast_fusion.14), channel_id=1, source_target_pairs={{0,8},{8,0},{16,24},{24,16},{1,9},{9,1},{17,25},{25,17},{2,10},{10... | collective-permute-start | bytes 786440 | tf_op jit(solution)/shard_map/cond/branch_1_fun/ppermute | solution.py:16
  70.9 5.6 %collective-permute-start.160 = (f32[1,128,256]{2,1,0:T(8,128)S(1)}, f32[1,128,256]{2,1,0:T(8,128)S(1)}, u32[]{:S(2)}, u32[]{:S(2)}) collective-permute-start(f32[1,128,256]{2,1,0:T(8,128)S(1)} %constant_dynamic-slice_fusion.14), channel_id=1, source_target_pairs={{0,16},{8,24},{16,0},{24,8},{1,17},{9,25},{17,1},{25,9},{2,18},{10... | collective-permute-start | bytes 393224 | tf_op jit(solution)/shard_map/cond/branch_1_fun/ppermute | solution.py:16
  72.8 4.4 %copy-start.34 = (f32[512,256]{1,0:T(8,128)}, f32[512,256]{1,0:T(8,128)S(1)}, u32[]{:S(2)}) copy-start(f32[512,256]{1,0:T(8,128)S(1)} %branch_1_fun.14) | copy-start | bytes 1572868 | tf_op jit(solution)/shard_map/cond
  72.9 4.4 %copy-start.36 = (f32[512,256]{1,0:T(8,128)}, f32[512,256]{1,0:T(8,128)S(1)}, u32[]{:S(2)}) copy-start(f32[512,256]{1,0:T(8,128)S(1)} %branch_1_fun.15) | copy-start | bytes 1572868 | tf_op jit(solution)/shard_map/cond

commit v2 on v1

--- a/solution.py
+++ b/solution.py
@@ -145,7 +145,7 @@
         return both, 0
     if first & 1:
         return both & ~1, 0
-    return both, both
+    return both, both & 1
 
 
 def before(first, second, state):
@@ -186,7 +186,7 @@
         if not crosses(second):
             last = move(held, "col", second)
         elif cols_by != both:
-            last = move(cols, "col", both)
+            last = move(last if cols_by else cols, "col", both ^ cols_by)
         last, next_acc = adagrad(last, next_acc, grad)
     else:
         later, later_acc = adagrad(held[half:], waiting, grad[half:])
@@ -218,7 +218,8 @@
     pairs = [(m, full) for m in range(1, full)]
     pairs += [(full, m) for m in range(full - 1, 0, -1)]
     pairs.insert(full - 1, pairs[full - 1])
-    which = plan[0] - plan[1] + (full - 1)
+    at = lax.iota(plan.dtype, 2)
+    which = jnp.sum(jnp.where(at == 0, plan + (full - 1), -plan))
 
     def by_plan(step, state):
         return lax.switch(which, [lambda s, a=a, b=b: step(a, b, s) for a, b in pairs], state)
@@ -236,7 +237,7 @@
     )
     grad, grad_rows = tile_grads(tiles[1], whole, held, rows_marginal, log_next)
     return lax.cond(
-        plan[0] >= lax.axis_size("col") // 2,
+        which >= (full + 1) // 2 - 1,
         lambda s: after(False, s),
         lambda s: after(True, s),
         (shard, shard_acc, held, held_acc, grad, grad_rows),

time: 77.5 us -> 80.2 us (1.035)
  waiting for transfers between devices: 45 us -> 47.2 us
  other arithmetic: 5.43 us -> 6.86 us
    ppermute x16, waiting for transfers between devices: 45 us -> 47.2 us  [move(): return lax.ppermute(value, axis, pairs)]
    slice x1 -> x0, local copies, waits for them, and re-layouts: 1.31 us -> none  [two_rounds(): which = plan[0] - plan[1] + (full - 1)]
    reduce_sum x0 -> x1, other arithmetic: none -> 1.29 us  [two_rounds(): which = jnp.sum(jnp.where(at == 0, plan + (full - 1), -plan))]
    squeeze x1, local copies, waits for them, and re-layouts: 0.17 us -> 1.17 us  [before(): counts[t].reshape(rows_block, tile_cols)]
    add x2, other arithmetic: 0.07 us -> 1.03 us  [row_sum_scatter(): blocks = keep + move(send, 'row', 1 << bit)]
  transfers between devices with their start and end apart: 16 -> 16, of which waited for: 8 -> 9; matrix products, arithmetic and copies ran while one was open for 8% -> 10% of each run, Pallas kernels for 0% -> 0%
where the time goes in v2:
time: 80.2 us; the launch traced here: 80.1 us
  waiting for transfers between devices  47.2 us (59%)
  starting transfers between devices  12.2 us (15%)
  Pallas kernels  7.17 us (9%)
  other arithmetic  6.86 us (9%)
  local copies, waits for them, and re-layouts  4.08 us (5%)
  between operations  2.02 us (3%)
    ppermute x16, waiting for transfers between devices, move(): return lax.ppermute(value, axis, pairs)  47.2 us
    ppermute x16, starting transfers between devices, move(): return lax.ppermute(value, axis, pairs)  12.2 us
    pallas_call x2, Pallas kernels, tile_grads(): pl.pallas_call(tile_kernel, out_shape=[jax.ShapeDtypeStruct(held.shape, j...  7.16 us
    sub x3, other arithmetic, adagrad(): return (param - learn_rate * grad / jnp.sqrt(accum), accum)  3.56 us
    another operation x1, local copies, waits for them, and re-layouts  1.76 us
  transfers between devices with their start and end apart: 16, of which 9 were waited for; matrix products, arithmetic and copies ran while one was open for 10% of the time, Pallas kernels for 0%

profile of v2, /device:TPU:8, one launch (start us, length us, event | category | flops | bytes accessed | tf_op | source)
XLA Modules:
  0.0 80.1 jit_solution(2612557713538769178)
XLA Ops:
  0.6 1.3 %fusion.45 = s32[]{:T(128)} fusion(s32[2]{0:T(128)} %param.43), kind=kLoop, calls=%fused_computation.301 | loop fusion | flops 9 | bytes 12 | tf_op jit(solution)/shard_map/reduce_sum | solution.py:222
  3.2 0.0 copy-start
  3.2 30.6 %conditional.3 = (f32[512,256]{1,0:T(8,128)}, f32[512,256]{1,0:T(8,128)}, f32[512,256]{1,0:T(8,128)}, f32[256,256]{1,0:T(8,128)}, f32[512,256]{1,0:T(8,128)S(1)}...) conditional(s32[]{:T(128)} %clamp.4, (f32[512,256]{1,0:T(8,128)}, ...), branch_computations={%region_1.2_spmd, %region_2.3_spmd, %region_3.4_spmd, %region_4.5_... | conditional | flops 786953 | bytes 829913280 | solution.py:225
  3.3 1.6 %collective-permute-start.38 = (f32[128,256]{1,0:T(8,128)}, f32[128,256]{1,0:T(8,128)S(1)}, u32[]{:S(2)}, u32[]{:S(2)}) collective-permute-start(f32[128,256]{1,0:T(8,128)} %bitcast.608), channel_id=1, source_target_pairs={{0,16},{8,24},{16,0},{24,8},{1,17},{9,25},{17,1},{25,9},{2,18},{10... | collective-permute-start | bytes 393224 | tf_op jit(solution)/shard_map/cond/branch_8_fun/ppermute | solution.py:16
  4.8 0.0 collective-permute-start.37
  4.8 2.5 %collective-permute-start.35 = (f32[512,256]{1,0:T(8,128)}, f32[512,256]{1,0:T(8,128)}, u32[]{:S(2)}, u32[]{:S(2)}) collective-permute-start(f32[512,256]{1,0:T(8,128)} %get-tuple-element.416), channel_id=1, source_target_pairs={{0,7},{1,6},{2,5},{3,4},{4,3},{5,2},{6,1},{7,0},{8,15},{9,14},{10,... | collective-permute-start | bytes 1572872 | tf_op jit(solution)/shard_map/cond/branch_8_fun/ppermute | solution.py:16
  7.4 2.5 %collective-permute-start.36 = (f32[512,256]{1,0:T(8,128)}, f32[512,256]{1,0:T(8,128)}, u32[]{:S(2)}, u32[]{:S(2)}) collective-permute-start(f32[512,256]{1,0:T(8,128)} %get-tuple-element.417), channel_id=1, source_target_pairs={{0,2},{1,3},{2,0},{3,1},{4,6},{5,7},{6,4},{7,5},{8,10},{9,11},{10,... | collective-permute-start | bytes 1572872 | tf_op jit(solution)/shard_map/cond/branch_8_fun/ppermute | solution.py:16
  9.9 1.8 %copy.92 = s32[2,1,512,1,512]{4,2,3,1,0:T(8,128)S(1)} copy(s32[2,1,512,1,512]{4,3,2,1,0:T(1,128)} %get-tuple-element.422) | data formatting | bytes 4194304 | tf_op jit(solution)/shard_map
  11.6 0.0 copy-start.48
  11.6 0.0 copy-start.13
  11.6 1.2 %slice_bitcast_fusion.16 = (s32[512,512]{1,0:T(8,128)S(1)}, s32[512,512]{1,0:T(8,128)}) fusion(s32[2,1,512,1,512]{4,2,3,1,0:T(8,128)S(1)} %copy.92), kind=kLoop, calls=%fused_computation.59 | loop fusion | bytes 4194304 | tf_op jit(solution)/shard_map/cond/branch_8_fun/reshape;cond/branch_8_fun/squeeze | solution.py:172
  12.8 0.0 collective-permute-done.38
  12.8 0.0 collective-permute-start.39
  12.8 0.0 copy-done.48
  12.8 0.2 collective-permute-start.41
  13.1 0.0 collective-permute-done.37
  13.1 0.0 collective-permute-start.40
  13.1 1.1 %collective-permute-done.39 = f32[128,256]{1,0:T(8,128)S(1)} collective-permute-done((f32[128,256]{1,0:T(8,128)S(1)}, f32[128,256]{1,0:T(8,128)S(1)}, u32[]{:S(2)}, u32[]{:S(2)}) %collective-permute-start.39) | collective-permute-done | bytes 131104 | tf_op jit(solution)/shard_map/cond/branch_8_fun/ppermute | solution.py:16
  14.2 0.0 copy-done.13
  14.3 17.3 %collective-permute-done.35.source = f32[512,256]{1,0:T(8,128)} collective-permute-done((f32[512,256]{1,0:T(8,128)}, f32[512,256]{1,0:T(8,128)}, u32[]{:S(2)}, u32[]{:S(2)}) %collective-permute-start.35) | collective-permute-done | bytes 524320 | tf_op jit(solution)/shard_map/cond/branch_8_fun/ppermute | solution.py:16
  31.7 2.1 %collective-permute-done.36.source = f32[512,256]{1,0:T(8,128)} collective-permute-done((f32[512,256]{1,0:T(8,128)}, f32[512,256]{1,0:T(8,128)}, u32[]{:S(2)}, u32[]{:S(2)}) %collective-permute-start.36) | collective-permute-done | bytes 524320 | tf_op jit(solution)/shard_map/cond/branch_8_fun/ppermute | solution.py:16
  33.8 0.0 collective-permute-done.41
  33.8 0.0 collective-permute-done.40
  33.8 1.0 %copy-done.39 = s32[512,512]{1,0:T(8,128)} copy-done((s32[512,512]{1,0:T(8,128)}, s32[512,512]{1,0:T(8,128)S(1)}, u32[]{:S(2)}) %copy-start.39) | copy-done | bytes 1048600
  34.8 0.0 copy-done
  34.9 0.0 copy-start.38
  34.9 3.6 %shard_map.119 = (f32[512,256]{1,0:T(8,128)S(1)}, f32[512,256]{1,0:T(8,128)S(1)}) custom-call(s32[512,512]{1,0:T(8,128)} %get-tuple-element.579.tile, f32[512,256]{1,0:T(8,128)S(1)} %get-tuple-element.580.whole, f32[512,256]{1,0:T(8,128)} %get-tuple-element.581.held, s32[1,512]{1,0:T(1,128)S(1)} %copy-done, f32[1,512]{1,0:T(1,128)} %get-tuple-element.582.log_c), custom_call_target="tpu_custom_call" | custom-call | flops 1207959552 | bytes 3145728 | tf_op jit(solution)/shard_map/pallas_call | solution.py:117
  38.5 0.0 copy-done.4
  38.5 0.0 copy-done.32
  38.5 0.0 copy-done.37
  38.5 0.0 copy-done.38
  38.5 29.9 %conditional.4 = (f32[128,256]{1,0:T(8,128)}, f32[128,256]{1,0:T(8,128)S(1)}, f32[512,256]{1,0:T(8,128)S(1)}, f32[512,256]{1,0:T(8,128)}, f32[512,256]{1,0:T(8,128)}) conditional(s32[]{:T(128)} %clamp.4, (f32[512,256]{1,0:T(8,128)S(1)}, f32[128,256]{1,0:T(8,128)S(1)}, f32[128,256]{1,0:T(8,128)S(1)}, ...), branch_computations={%region_14.15_spmd, %region_15.16_spmd, %region_16.17_spmd, %regio... | conditional | flops 1966103 | bytes 818088640 | solution.py:225
  38.6 0.1 collective-permute-start.121
  38.7 0.4 collective-permute-start.126
  39.1 3.0 %collective-permute-start.127 = (f32[512,256]{1,0:T(8,128)S(1)}, f32[512,256]{1,0:T(8,128)S(1)}, u32[]{:S(2)}, u32[]{:S(2)}) collective-permute-start(f32[512,256]{1,0:T(8,128)S(1)} %get-tuple-element.518), channel_id=1, source_target_pairs={{0,5},{1,4},{2,7},{3,6},{4,1},{5,0},{6,3},{7,2},{8,13},{9,12},{10,... | collective-permute-start | bytes 1572872 | tf_op jit(solution)/shard_map/cond/branch_8_fun/ppermute | solution.py:16
  42.1 0.0 collective-permute-done.121
  42.1 1.0 %bitcast_add_fusion.16 = f32[2,128,256]{2,1,0:T(8,128)S(1)} fusion(f32[2,128,256]{2,1,0:T(8,128)} %collective-permute-done.121, f32[2,2,128,256]{3,2,1,0:T(8,128)S(1)} %bitcast.557, s32[]{:T(128)S(6)} %select_n.453), kind=kLoop, calls=%fused_computation.219 | loop fusion | flops 65536 | bytes 786436 | tf_op jit(solution)/shard_map/cond/branch_8_fun/add | solution.py:36
  43.1 0.6 collective-permute-start.122
  43.7 4.9 %collective-permute-done.122 = f32[1,128,256]{2,1,0:T(8,128)S(1)} collective-permute-done((f32[1,128,256]{2,1,0:T(8,128)S(1)}, f32[1,128,256]{2,1,0:T(8,128)S(1)}, u32[]{:S(2)}, u32[]{:S(2)}) %collective-permute-start.122) | collective-permute-done | bytes 131104 | tf_op jit(solution)/shard_map/cond/branch_8_fun/ppermute | solution.py:16
  48.7 0.0 copy-start.26
  48.7 0.6 collective-permute-start.124
  49.3 0.0 collective-permute-start.123
  49.3 4.4 %collective-permute-done.124 = f32[128,256]{1,0:T(8,128)S(1)} collective-permute-done((f32[128,256]{1,0:T(8,128)S(1)}, f32[128,256]{1,0:T(8,128)S(1)}, u32[]{:S(2)}, u32[]{:S(2)}) %collective-permute-start.124) | collective-permute-done | bytes 131104 | tf_op jit(solution)/shard_map/cond/branch_8_fun/ppermute | solution.py:16
  53.8 0.0 collective-permute-start.125
  53.8 7.9 %collective-permute-done.126 = f32[512,256]{1,0:T(8,128)S(1)} collective-permute-done((f32[512,256]{1,0:T(8,128)S(1)}, f32[512,256]{1,0:T(8,128)S(1)}, u32[]{:S(2)}, u32[]{:S(2)}) %collective-permute-start.126) | collective-permute-done | bytes 524320 | tf_op jit(solution)/shard_map/cond/branch_8_fun/ppermute | solution.py:16
  61.6 4.3 %collective-permute-done.127 = f32[512,256]{1,0:T(8,128)S(1)} collective-permute-done((f32[512,256]{1,0:T(8,128)S(1)}, f32[512,256]{1,0:T(8,128)S(1)}, u32[]{:S(2)}, u32[]{:S(2)}) %collective-permute-start.127) | collective-permute-done | bytes 524320 | tf_op jit(solution)/shard_map/cond/branch_8_fun/ppermute | solution.py:16
  65.9 2.2 %multiply_subtract_fusion.11 = (f32[512,256]{1,0:T(8,128)}, f32[512,256]{1,0:T(8,128)}) fusion(f32[512,256]{1,0:T(8,128)S(1)} %collective-permute-done.126, f32[512,256]{1,0:T(8,128)S(1)} %collective-permute-done.127, f32[512,256]{1,0:T(8,128)} %get-tuple-element.519), kind=kLoop, calls=%fused_computation.217 | loop fusion | flops 655360 | bytes 2621440 | tf_op jit(solution)/shard_map/cond/branch_8_fun/sub | solution.py:21
  68.1 0.0 collective-permute-done.123
  68.1 0.0 collective-permute-done.125
  68.1 0.0 copy-done.26
  68.5 0.0 copy-start.31
  68.5 3.5 %shard_map.120 = (f32[512,256]{1,0:T(8,128)S(1)}, f32[512,256]{1,0:T(8,128)S(1)}) custom-call(s32[512,512]{1,0:T(8,128)} %copy-done.39, f32[512,256]{1,0:T(8,128)S(1)} %get-tuple-element.588.whole, f32[512,256]{1,0:T(8,128)} %get-tuple-element.589.held, s32[1,512]{1,0:T(1,128)S(1)} %copy-done, f32[1,512]{1,0:T(1,128)} %get-tuple-element.590.log_c), custom_call_target="tpu_custom_call" | custom-call | flops 1207959552 | bytes 3145728 | tf_op jit(solution)/shard_map/pallas_call | solution.py:117
  72.0 0.0 copy-done.31
  72.0 8.1 %conditional.5 = (f32[1,128,256]{2,1,0:T(8,128)}, f32[1,128,256]{2,1,0:T(8,128)}, f32[1,1,512,256]{3,2,1,0:T(8,128)}, f32[1,1,512,256]{3,2,1,0:T(8,128)}) conditional(s32[]{:T(128)} %convert_element_type.42, (f32[512,256]{1,0:T(8,128)S(1)}, f32[128,256]{1,0:T(8,128)S(1)}, f32[128,256]{1,0:T(8,128)S(1)}, f32[512,256]{1,0:T(8,128)S(1)}, ...), branch_computations={%region_27.28_spmd, %region_28.29_spmd} | conditional | flops 1048597 | bytes 812845440 | solution.py:239
  72.1 0.1 collective-permute-start.160
  72.2 1.5 %collective-permute-done.160 = f32[2,128,256]{2,1,0:T(8,128)S(1)} collective-permute-done((f32[2,128,256]{2,1,0:T(8,128)S(1)}, f32[2,128,256]{2,1,0:T(8,128)S(1)}, u32[]{:S(2)}, u32[]{:S(2)}) %collective-permute-start.160) | collective-permute-done | bytes 262176 | tf_op jit(solution)/shard_map/cond/branch_1_fun/ppermute | solution.py:16
  73.8 0.6 collective-permute-start.161
  74.4 1.3 %multiply_subtract_fusion.17 = (f32[512,256]{1,0:T(8,128)S(1)}, f32[512,256]{1,0:T(8,128)S(1)}) fusion(f32[512,256]{1,0:T(8,128)} %get-tuple-element.553, f32[512,256]{1,0:T(8,128)S(1)} %get-tuple-element.554, f32[512,256]{1,0:T(8,128)} %get-tuple-element.555), kind=kLoop, calls=%fused_computation.289 | loop fusion | flops 655360 | bytes 2621440 | tf_op jit(solution)/shard_map/cond/branch_1_fun/sub | solution.py:21
  75.7 0.0 copy-start.34
  75.7 0.0 copy-start.36
  75.7 3.6 %collective-permute-done.161 = f32[1,128,256]{2,1,0:T(8,128)S(1)} collective-permute-done((f32[1,128,256]{2,1,0:T(8,128)S(1)}, f32[1,128,256]{2,1,0:T(8,128)S(1)}, u32[]{:S(2)}, u32[]{:S(2)}) %collective-permute-start.161) | collective-permute-done | bytes 131104 | tf_op jit(solution)/shard_map/cond/branch_1_fun/ppermute | solution.py:16
  79.4 0.7 fusion.44
  80.1 0.0 copy-done.34
  80.1 0.0 copy-done.36
  (25 shorter events, 0.4 us)
Async XLA Ops:
  3.2 31.6 %copy-start = (s32[1,512]{1,0:T(1,128)S(1)}, s32[1,512]{1,0:T(1,128)}, u32[]{:S(2)}) copy-start(s32[1,512]{1,0:T(1,128)} %rows_marginal.3) | copy-start | bytes 6148
  3.3 9.5 %collective-permute-start.38 = (f32[128,256]{1,0:T(8,128)}, f32[128,256]{1,0:T(8,128)S(1)}, u32[]{:S(2)}, u32[]{:S(2)}) collective-permute-start(f32[128,256]{1,0:T(8,128)} %bitcast.608), channel_id=1, source_target_pairs={{0,16},{8,24},{16,0},{24,8},{1,17},{9,25},{17,1},{25,9},{2,18},{10... | collective-permute-start | bytes 393224 | tf_op jit(solution)/shard_map/cond/branch_8_fun/ppermute | solution.py:16
  4.8 8.2 %collective-permute-start.37 = (f32[128,256]{1,0:T(8,128)}, f32[128,256]{1,0:T(8,128)S(1)}, u32[]{:S(2)}, u32[]{:S(2)}) collective-permute-start(f32[128,256]{1,0:T(8,128)} %bitcast.609), channel_id=1, source_target_pairs={{0,8},{8,0},{16,24},{24,16},{1,9},{9,1},{17,25},{25,17},{2,10},{10... | collective-permute-start | bytes 393224 | tf_op jit(solution)/shard_map/cond/branch_8_fun/ppermute | solution.py:16
  4.8 26.8 %collective-permute-start.35 = (f32[512,256]{1,0:T(8,128)}, f32[512,256]{1,0:T(8,128)}, u32[]{:S(2)}, u32[]{:S(2)}) collective-permute-start(f32[512,256]{1,0:T(8,128)} %get-tuple-element.416), channel_id=1, source_target_pairs={{0,7},{1,6},{2,5},{3,4},{4,3},{5,2},{6,1},{7,0},{8,15},{9,14},{10,... | collective-permute-start | bytes 1572872 | tf_op jit(solution)/shard_map/cond/branch_8_fun/ppermute | solution.py:16
  7.4 26.4 %collective-permute-start.36 = (f32[512,256]{1,0:T(8,128)}, f32[512,256]{1,0:T(8,128)}, u32[]{:S(2)}, u32[]{:S(2)}) collective-permute-start(f32[512,256]{1,0:T(8,128)} %get-tuple-element.417), channel_id=1, source_target_pairs={{0,2},{1,3},{2,0},{3,1},{4,6},{5,7},{6,4},{7,5},{8,10},{9,11},{10,... | collective-permute-start | bytes 1572872 | tf_op jit(solution)/shard_map/cond/branch_8_fun/ppermute | solution.py:16
  11.6 1.2 %copy-start.48 = (s32[512]{0:T(512)S(1)}, s32[512]{0:T(512)}, u32[]{:S(2)}) copy-start(s32[512]{0:T(512)} %get-tuple-element.425) | copy-start | bytes 6148 | tf_op jit(solution)/shard_map/cond
  11.6 2.5 %copy-start.13 = (f32[1,128,256]{2,1,0:T(8,128)S(1)}, f32[1,128,256]{2,1,0:T(8,128)}, u32[]{:S(2)}) copy-start(f32[1,128,256]{2,1,0:T(8,128)} %get-tuple-element.418) | copy-start | bytes 393220 | tf_op jit(solution)/shard_map/cond
  12.8 1.3 %collective-permute-start.39 = (f32[128,256]{1,0:T(8,128)S(1)}, f32[128,256]{1,0:T(8,128)S(1)}, u32[]{:S(2)}, u32[]{:S(2)}) collective-permute-start(f32[128,256]{1,0:T(8,128)S(1)} %collective-permute-done.38), channel_id=1, source_target_pairs={{0,8},{8,0},{16,24},{24,16},{1,9},{9,1},{17,25},{25,17},{2,10},{10... | collective-permute-start | bytes 393224 | tf_op jit(solution)/shard_map/cond/branch_8_fun/ppermute | solution.py:16
  12.8 21.0 %collective-permute-start.41 = (f32[512]{0:T(512)S(1)}, f32[512]{0:T(512)}, u32[]{:S(2)}, u32[]{:S(2)}) collective-permute-start(f32[512]{0:T(512)S(1)} %convert_log_fusion.8), channel_id=1, source_target_pairs={{0,2},{1,3},{2,0},{3,1},{4,6},{5,7},{6,4},{7,5},{8,10},{9,11},{10,... | collective-permute-start | bytes 6152 | tf_op jit(solution)/shard_map/cond/branch_8_fun/ppermute | solution.py:16
  13.1 20.8 %collective-permute-start.40 = (f32[512]{0:T(512)S(1)}, f32[512]{0:T(512)}, u32[]{:S(2)}, u32[]{:S(2)}) collective-permute-start(f32[512]{0:T(512)S(1)} %convert_log_fusion.8), channel_id=1, source_target_pairs={{0,7},{1,6},{2,5},{3,4},{4,3},{5,2},{6,1},{7,0},{8,15},{9,14},{10,... | collective-permute-start | bytes 6152 | tf_op jit(solution)/shard_map/cond/branch_8_fun/ppermute | solution.py:16
  33.8 1.0 %copy-start.39 = (s32[512,512]{1,0:T(8,128)}, s32[512,512]{1,0:T(8,128)S(1)}, u32[]{:S(2)}) copy-start(s32[512,512]{1,0:T(8,128)S(1)} %get-tuple-element.578.tile) | copy-start | bytes 3145732
  34.8 3.6 %copy-start.4 = (f32[1,128,256]{2,1,0:T(8,128)S(1)}, f32[1,128,256]{2,1,0:T(8,128)}, u32[]{:S(2)}) copy-start(f32[1,128,256]{2,1,0:T(8,128)} %param.36) | copy-start | bytes 393220
  34.8 3.6 %copy-start.32 = (f32[1,128,256]{2,1,0:T(8,128)S(1)}, f32[1,128,256]{2,1,0:T(8,128)}, u32[]{:S(2)}) copy-start(f32[1,128,256]{2,1,0:T(8,128)} %param.37) | copy-start | bytes 393220
  34.9 3.7 %copy-start.37 = (f32[1,1,512,256]{3,2,1,0:T(8,128)S(1)}, f32[1,1,512,256]{3,2,1,0:T(8,128)}, u32[]{:S(2)}) copy-start(f32[1,1,512,256]{3,2,1,0:T(8,128)} %param.40) | copy-start | bytes 1572868
  34.9 3.7 %copy-start.38 = (f32[1,1,512,256]{3,2,1,0:T(8,128)S(1)}, f32[1,1,512,256]{3,2,1,0:T(8,128)}, u32[]{:S(2)}) copy-start(f32[1,1,512,256]{3,2,1,0:T(8,128)} %param.39) | copy-start | bytes 1572868
  38.6 3.5 %collective-permute-start.121 = (f32[2,128,256]{2,1,0:T(8,128)S(1)}, f32[2,128,256]{2,1,0:T(8,128)}, u32[]{:S(2)}, u32[]{:S(2)}) collective-permute-start(f32[2,128,256]{2,1,0:T(8,128)S(1)} %dynamic-slice_bitcast_fusion.8), channel_id=1, source_target_pairs={{0,8},{8,0},{16,24},{24,16},{1,9},{9,1},{17,25},{25,17},{2,10},{10... | collective-permute-start | bytes 786440 | tf_op jit(solution)/shard_map/cond/branch_8_fun/ppermute | solution.py:16
  38.7 22.9 %collective-permute-start.126 = (f32[512,256]{1,0:T(8,128)S(1)}, f32[512,256]{1,0:T(8,128)S(1)}, u32[]{:S(2)}, u32[]{:S(2)}) collective-permute-start(f32[512,256]{1,0:T(8,128)S(1)} %get-tuple-element.517), channel_id=1, source_target_pairs={{0,2},{1,3},{2,0},{3,1},{4,6},{5,7},{6,4},{7,5},{8,10},{9,11},{10,... | collective-permute-start | bytes 1572872 | tf_op jit(solution)/shard_map/cond/branch_8_fun/ppermute | solution.py:16
  39.1 26.8 %collective-permute-start.127 = (f32[512,256]{1,0:T(8,128)S(1)}, f32[512,256]{1,0:T(8,128)S(1)}, u32[]{:S(2)}, u32[]{:S(2)}) collective-permute-start(f32[512,256]{1,0:T(8,128)S(1)} %get-tuple-element.518), channel_id=1, source_target_pairs={{0,5},{1,4},{2,7},{3,6},{4,1},{5,0},{6,3},{7,2},{8,13},{9,12},{10,... | collective-permute-start | bytes 1572872 | tf_op jit(solution)/shard_map/cond/branch_8_fun/ppermute | solution.py:16
  43.1 5.5 %collective-permute-start.122 = (f32[1,128,256]{2,1,0:T(8,128)S(1)}, f32[1,128,256]{2,1,0:T(8,128)S(1)}, u32[]{:S(2)}, u32[]{:S(2)}) collective-permute-start(f32[1,128,256]{2,1,0:T(8,128)S(1)} %constant_dynamic-slice_fusion.8), channel_id=1, source_target_pairs={{0,16},{8,24},{16,0},{24,8},{1,17},{9,25},{17,1},{25,9},{2,18},{10... | collective-permute-start | bytes 393224 | tf_op jit(solution)/shard_map/cond/branch_8_fun/ppermute | solution.py:16
  48.7 19.3 %copy-start.26 = (f32[128,256]{1,0:T(8,128)}, f32[128,256]{1,0:T(8,128)S(1)}, u32[]{:S(2)}) copy-start(f32[128,256]{1,0:T(8,128)S(1)} %get-tuple-element.869) | copy-start | bytes 393220 | tf_op jit(solution)/shard_map/cond
  48.7 5.0 %collective-permute-start.124 = (f32[128,256]{1,0:T(8,128)S(1)}, f32[128,256]{1,0:T(8,128)S(1)}, u32[]{:S(2)}, u32[]{:S(2)}) collective-permute-start(f32[128,256]{1,0:T(8,128)S(1)} %get-tuple-element.869), channel_id=1, source_target_pairs={{0,16},{8,24},{16,0},{24,8},{1,17},{9,25},{17,1},{25,9},{2,18},{10... | collective-permute-start | bytes 393224 | tf_op jit(solution)/shard_map/cond/branch_8_fun/ppermute | solution.py:16
  49.3 18.7 %collective-permute-start.123 = (f32[128,256]{1,0:T(8,128)S(1)}, f32[128,256]{1,0:T(8,128)S(1)}, u32[]{:S(2)}, u32[]{:S(2)}) collective-permute-start(f32[128,256]{1,0:T(8,128)S(1)} %get-tuple-element.869), channel_id=1, source_target_pairs={{0,8},{8,0},{16,24},{24,16},{1,9},{9,1},{17,25},{25,17},{2,10},{10... | collective-permute-start | bytes 393224 | tf_op jit(solution)/shard_map/cond/branch_8_fun/ppermute | solution.py:16
  53.8 14.3 %collective-permute-start.125 = (f32[128,256]{1,0:T(8,128)S(1)}, f32[128,256]{1,0:T(8,128)S(1)}, u32[]{:S(2)}, u32[]{:S(2)}) collective-permute-start(f32[128,256]{1,0:T(8,128)S(1)} %collective-permute-done.124), channel_id=1, source_target_pairs={{0,8},{8,0},{16,24},{24,16},{1,9},{9,1},{17,25},{25,17},{2,10},{10... | collective-permute-start | bytes 393224 | tf_op jit(solution)/shard_map/cond/branch_8_fun/ppermute | solution.py:16
  68.5 3.6 %copy-start.31 = (f32[128,256]{1,0:T(8,128)S(1)}, f32[128,256]{1,0:T(8,128)}, u32[]{:S(2)}) copy-start(f32[128,256]{1,0:T(8,128)} %get-tuple-element.593) | copy-start | bytes 393220
  72.1 1.6 %collective-permute-start.160 = (f32[2,128,256]{2,1,0:T(8,128)S(1)}, f32[2,128,256]{2,1,0:T(8,128)S(1)}, u32[]{:S(2)}, u32[]{:S(2)}) collective-permute-start(f32[2,128,256]{2,1,0:T(8,128)S(1)} %dynamic-slice_bitcast_fusion.14), channel_id=1, source_target_pairs={{0,8},{8,0},{16,24},{24,16},{1,9},{9,1},{17,25},{25,17},{2,10},{10... | collective-permute-start | bytes 786440 | tf_op jit(solution)/shard_map/cond/branch_1_fun/ppermute | solution.py:16
  73.8 5.6 %collective-permute-start.161 = (f32[1,128,256]{2,1,0:T(8,128)S(1)}, f32[1,128,256]{2,1,0:T(8,128)S(1)}, u32[]{:S(2)}, u32[]{:S(2)}) collective-permute-start(f32[1,128,256]{2,1,0:T(8,128)S(1)} %constant_dynamic-slice_fusion.14), channel_id=1, source_target_pairs={{0,16},{8,24},{16,0},{24,8},{1,17},{9,25},{17,1},{25,9},{2,18},{10... | collective-permute-start | bytes 393224 | tf_op jit(solution)/shard_map/cond/branch_1_fun/ppermute | solution.py:16
  75.7 4.4 %copy-start.34 = (f32[512,256]{1,0:T(8,128)}, f32[512,256]{1,0:T(8,128)S(1)}, u32[]{:S(2)}) copy-start(f32[512,256]{1,0:T(8,128)S(1)} %branch_1_fun.14) | copy-start | bytes 1572868 | tf_op jit(solution)/shard_map/cond
  75.7 4.4 %copy-start.36 = (f32[512,256]{1,0:T(8,128)}, f32[512,256]{1,0:T(8,128)S(1)}, u32[]{:S(2)}) copy-start(f32[512,256]{1,0:T(8,128)S(1)} %branch_1_fun.15) | copy-start | bytes 1572868 | tf_op jit(solution)/shard_map/cond
